TPU v7x, 32 devices: a whole 2x2x4 slice. The times are simulated.
32 devices in a mesh: blk: 4 (over y, x), seq: 8 (over z, core).
Axes of the slice: x: 2, y: 2, z: 4, core: 2. Of those that a mesh axis runs over, the one named last changes fastest.
Arguments:
- tokens: bfloat16 [16, 2048, 768], P('seq', 'blk'), may hold values from -6 to 6
- seq_len: int32 [16], P('seq'), may hold values from 1024 to 2048, as said below
- ln1_gain: bfloat16 [768], P(('blk', 'seq')), may hold values from 0.5 to 1.5
- ln1_shift: bfloat16 [768], P(('blk', 'seq')), may hold values from -2.5 to 2.5
- w_qkv: bfloat16 [768, 2304], P(('blk', 'seq')), may hold values from -0.21875 to 0.21875
- w_out: bfloat16 [768, 768], P(('blk', 'seq')), may hold values from -2.5 to 2.5
- ln2_gain: bfloat16 [768], P(('blk', 'seq')), may hold values from 0.5 to 1.5
- ln2_shift: bfloat16 [768], P(('blk', 'seq')), may hold values from -2.5 to 2.5
- w_up: bfloat16 [768, 3072], P(('blk', 'seq')), may hold values from -0.21875 to 0.21875
- w_down: bfloat16 [3072, 768], P(('blk', 'seq')), may hold values from -0.109375 to 0.109375
- cotangent: bfloat16 [16, 2048, 768], P('seq', 'blk'), may hold values from -6 to 6
Outputs:
- output: bfloat16 [16, 2048, 768], P('seq', 'blk')
- grad_tokens: float32 [16, 2048, 768], P('seq', 'blk')
- grad_ln1_gain: float32 [768], P(('blk', 'seq'))
- grad_ln1_shift: float32 [768], P(('blk', 'seq'))
- grad_w_qkv: float32 [768, 2304], P(('blk', 'seq'))
- grad_w_out: float32 [768, 768], P(('blk', 'seq'))
- grad_ln2_gain: float32 [768], P(('blk', 'seq'))
- grad_ln2_shift: float32 [768], P(('blk', 'seq'))
- grad_w_up: float32 [768, 3072], P(('blk', 'seq'))
- grad_w_down: float32 [3072, 768], P(('blk', 'seq'))
Inputs may be any that keep to these rules, and one draw needn't show every extreme that they name: `seq_len`: positions at or beyond a sequence's length are padding; in every draw some sequence has exactly 2048 positions and some exactly 1024.
All inputs are finite; a program needn't handle non-finite values.
Results may differ from a plain program's by a relative error of at most 0.02.
Values may be sent and summed in bfloat16 or wider, within the bound.
A program may use at most 448 MiB of HBM per device.

v0:
```python
import functools

import jax
import jax.numpy as jnp
from jax import lax
from jax.experimental import pallas as pl
from jax.experimental.pallas import tpu as pltpu
from jax.sharding import PartitionSpec as P

HEADS = 12
VMEM_LIMIT = 60 * 2**20


MESH = pl.DeviceIdType.MESH
DMA = pltpu.SemaphoreType.DMA
ANYWHERE = pl.BlockSpec(memory_space=pl.ANY)


class Place:
    def __init__(self, blocks, lanes, seqs):
        self.blocks, self.depth, self.seqs = blocks, lanes // 2, seqs
        self.share = blocks // seqs
        self.per_part = blocks // self.share
        self.bits = max(1, blocks.bit_length() - 1)
        self.blk = lax.axis_index("blk")
        lane = lax.axis_index("seq")
        self.z, self.core = lane // 2, lane % 2
        flat = self.blk * 2 + self.core
        self.seq, self.part = flat // self.share, flat % self.share
        self.home = self.seq // seqs
        self.other = lax.rem(self.blk * 2 + 1 - self.core, self.share)

    def at(self, blk, z, core):
        return (blk, z * 2 + core)

    def sibling(self):
        return self.at(self.blk, self.z, 1 - self.core)

    def peers(self, along_z, along_blk):
        out = [self.sibling()]
        if along_z:
            out += [self.at(self.blk, lax.rem(self.z + k, self.depth), self.core) for k in range(1, self.depth)]
        if along_blk:
            for m in range(1, self.blocks):
                out += [self.at(self.blk ^ m, self.z, 0), self.at(self.blk ^ m, self.z, 1)]
        return out

    def bit(self, part, step):
        return 1 << ((part + step) % self.bits)

    def widen(self, k):
        masks, out, seen = [0], [], 0
        for t in range(self.bits):
            bit = self.bit(k, t)
            out.append((bit, list(masks), seen))
            seen += len(masks)
            masks += [m ^ bit for m in masks]
        return out

    def narrow(self, k):
        out, seen = [], 0
        for t in range(self.bits):
            masks = [0]
            for u in range(t + 1, self.bits):
                masks += [m ^ self.bit(k, u) for m in masks]
            out.append((self.bit(k, t), masks, seen))
            seen += len(masks)
        return out


def greet(devices):
    barrier = pltpu.get_barrier_semaphore()
    for device in devices:
        pl.semaphore_signal(barrier, inc=1, device_id=device, device_id_type=MESH)
    pl.semaphore_wait(barrier, len(devices))


def send(src, dst, send_sem, recv_sem, device):
    pltpu.make_async_remote_copy(
        src_ref=src, dst_ref=dst, send_sem=send_sem, recv_sem=recv_sem, device_id=device, device_id_type=MESH
    ).start()


def arrived(ref, sem):
    pltpu.make_async_copy(ref, ref, sem).wait()


class Fold:
    def __init__(self, place, kinds, grads, rows_in, sums, rows_out, scratch):
        self.place, self.kinds, self.grads = place, kinds, grads
        self.rows_in, self.sums, self.rows_out = rows_in, sums, rows_out
        self.count, self.moves = len(kinds), len(rows_in)
        n = self.count
        self.held, self.near, self.wide, self.tall = (scratch[i * n : i * n + n] for i in range(4))
        self.m_s, self.m_r, self.z_s, self.z_r, self.b_s, self.b_r, self.c_s, self.c_r, self.loc = scratch[4 * n :]
        self.order = list(range(1, place.depth)) + [0]
        self.units = [(a, k) for a in range(n) for k in self.order]

    @staticmethod
    def scratch(sizes, chunks, types, kinds, moves):
        blocks, lanes, seqs = sizes
        depth, share, count = lanes // 2, blocks // seqs, len(chunks)
        out = [pltpu.VMEM((blocks, depth) + c, t) for c, t in zip(chunks, types)]
        out += [
            pltpu.VMEM((1, 1, 8, 128) if kind == "columns" else (blocks, depth) + c, t)
            for c, t, kind in zip(chunks, types, kinds)
        ]
        out += [pltpu.VMEM((depth, blocks - 1) + c, t) for c, t in zip(chunks, types)]
        out += [pltpu.VMEM((depth - 1,) + c, t) for c, t in zip(chunks, types)]
        return out + [
            DMA((max(1, moves), blocks // share)),
            DMA((max(1, moves), seqs)),
            DMA((count, depth - 1)),
            DMA((count, depth - 1)),
            DMA((count, depth, blocks - 1)),
            DMA((count, depth, blocks - 1)),
            DMA((count, depth)),
            DMA((count, depth)),
            DMA((count + 1, max(depth, moves))),
        ]

    def level(self, k):
        return lax.rem(self.place.z + k, self.place.depth)

    def greet(self):
        greet(self.place.peers(True, True))

    def clear(self):
        place = self.place
        for a in range(self.count):
            if self.kinds[a] == "columns" and place.share > 2:
                held = self.held[a]
                for g in range(place.share):

                    @pl.when((g != place.part) & (g != place.other))
                    def _(held=held, g=g):
                        held[:, :, g] = jnp.zeros(held.shape[:2] + held.shape[3:], held.dtype)

    def start(self, a, k):
        place = self.place
        if self.kinds[a] == "columns":
            mine = there = self.held[a].at[:, self.level(k), place.part]
        else:
            mine = self.held[a].at[:, self.level(k)]
            there = self.near[a].at[:, self.level(k)]
        theirs = self.grads[a].at[:, self.level(k), 1 - place.core]
        send(theirs, there, self.c_s.at[a, k], self.c_r.at[a, k], place.sibling())
        pltpu.make_async_copy(self.grads[a].at[:, self.level(k), place.core], mine, self.loc.at[a, k]).start()

    def add(self, into, second):
        total = into[...].astype(jnp.float32) + second[...].astype(jnp.float32)
        into[...] = total.astype(into.dtype)

    def forward(self, a, k, t):
        place = self.place
        bit, masks, seen = place.narrow(k)[t]
        for n, m in enumerate(masks):
            sems = self.b_s.at[a, k, seen + n], self.b_r.at[a, k, seen + n]
            block = self.held[a].at[place.blk ^ bit ^ m, self.level(k)]
            send(block, self.wide[a].at[k, seen + n], *sems, place.at(place.blk ^ bit, place.z, place.core))

    def join(self, a, k):
        place = self.place
        if self.kinds[a] == "columns":
            arrived(self.held[a].at[:, self.level(k), place.part], self.loc.at[a, k])
            arrived(self.held[a].at[:, self.level(k), place.other], self.c_r.at[a, k])
        else:
            arrived(self.held[a].at[:, self.level(k)], self.loc.at[a, k])
            arrived(self.near[a].at[:, self.level(k)], self.c_r.at[a, k])

            def one(b, _):
                self.add(self.held[a].at[b, self.level(k)], self.near[a].at[b, self.level(k)])
                return 0

            lax.fori_loop(0, place.blocks, one, 0)
        self.forward(a, k, 0)

    def step(self, a, k, t):
        place = self.place
        bit, masks, seen = place.narrow(k)[t]
        for n, m in enumerate(masks):
            arrived(self.wide[a].at[k, seen + n], self.b_r.at[a, k, seen + n])
            self.add(self.held[a].at[place.blk ^ m, self.level(k)], self.wide[a].at[k, seen + n])
        if t + 1 < place.bits:
            self.forward(a, k, t + 1)
        elif k > 0:
            sems = self.z_s.at[a, k - 1], self.z_r.at[a, k - 1]
            block = self.held[a].at[place.blk, self.level(k)]
            send(block, self.tall[a].at[k - 1], *sems, place.at(place.blk, self.level(k), place.core))

    def total(self, a):
        place = self.place
        value = self.held[a][place.blk, place.z].astype(jnp.float32)
        for k in range(1, place.depth):
            arrived(self.tall[a].at[k - 1], self.z_r.at[a, k - 1])
            value = value + self.tall[a][k - 1].astype(jnp.float32)
        self.sums[a][...] = value

    def rows(self, j):
        place = self.place
        slot = lax.rem(place.seq, place.seqs)
        for t in range(place.per_part):
            source = place.part * place.per_part + t
            mine = (source == place.blk) & (place.home == place.core)

            @pl.when(mine)
            def _(t=t):
                pltpu.make_async_copy(self.rows_in[j].at[t], self.rows_out[j].at[slot], self.loc.at[self.count, j]).start()

            @pl.when(jnp.logical_not(mine))
            def _(t=t, source=source):
                sems = self.m_s.at[j, t], self.m_r.at[j, slot]
                send(self.rows_in[j].at[t], self.rows_out[j].at[slot], *sems, place.at(source, place.z, place.home))

    def finish(self):
        place = self.place
        for a, k in self.units:
            if self.kinds[a] == "columns":
                arrived(self.held[a].at[:, 0, 0], self.c_s.at[a, k])
            else:
                arrived(self.held[a].at[:, 0], self.c_s.at[a, k])
            for n in range(place.blocks - 1):
                arrived(self.held[a].at[0, 0], self.b_s.at[a, k, n])
            if k > 0:
                arrived(self.held[a].at[0, 0], self.z_s.at[a, k - 1])
        for j in range(self.moves):
            for t in range(place.per_part):
                mine = (place.part * place.per_part + t == place.blk) & (place.home == place.core)

                @pl.when(mine)
                def _(j=j, t=t):
                    arrived(self.rows_in[j].at[t], self.loc.at[self.count, j])

                @pl.when(jnp.logical_not(mine))
                def _(j=j, t=t):
                    arrived(self.rows_in[j].at[t], self.m_s.at[j, t])

            for i in range(place.seqs):
                owner = (place.core * place.seqs + i) * place.share + place.blk // place.per_part

                @pl.when(owner != place.blk * 2 + place.core)
                def _(j=j, i=i):
                    arrived(self.rows_out[j].at[i], self.m_r.at[j, i])


def fold_shapes(sizes, grads, kinds, rows):
    blocks, _, seqs = sizes
    share = blocks // seqs
    chunks = [((share,) if kind == "columns" else ()) + g.shape[3:] for g, kind in zip(grads, kinds)]
    scratch = Fold.scratch(sizes, chunks, [g.dtype for g in grads], kinds, len(rows))
    out = [jax.ShapeDtypeStruct(c, jnp.float32) for c in chunks]
    moved = [jax.ShapeDtypeStruct((seqs,) + r.shape[1:], r.dtype) for r in rows]
    return out, moved, scratch


def dot_nt(left, right):
    return lax.dot_general(left, right, (((1,), (1,)), ((), ())), preferred_element_type=jnp.float32)


def dot_nn(left, right):
    return lax.dot_general(left, right, (((1,), (0,)), ((), ())), preferred_element_type=jnp.float32)


def split_heads(dst, src):
    low = lax.broadcasted_iota(jnp.int32, src.shape, 1) < 64
    dst[0] = jnp.where(low, src, jnp.zeros_like(src))
    dst[1] = jnp.where(low, jnp.zeros_like(src), src)


def causal(bk, bq, kj, qi):
    kpos = kj * bk + lax.broadcasted_iota(jnp.int32, (bk, bq), 0)
    qpos = qi * bq + lax.broadcasted_iota(jnp.int32, (bk, bq), 1)
    return kpos <= qpos


def plan(tasks, points):
    out = {}
    for where, call in tasks:
        out.setdefault(min(points - 1, int(where * points)), []).append(call)
    return out


def pump(todo, point):
    for at, calls in todo.items():

        @pl.when(point == at)
        def _(calls=calls):
            for call in calls:
                call()


class Total:
    def __init__(self, place, stages, from_z, from_blk, from_core, sems):
        self.place, self.stages = place, stages
        self.from_z, self.from_blk, self.from_core = from_z, from_blk, from_core
        self.z_s, self.z_r, self.b_s, self.b_r, self.c_s, self.c_r = sems

    @staticmethod
    def scratch(sizes, shape):
        blocks, lanes, _ = sizes
        depth, bits = lanes // 2, max(1, blocks.bit_length() - 1)
        return [
            pltpu.VMEM((2 + bits,) + shape, jnp.float32),
            pltpu.VMEM((depth - 1,) + shape, jnp.float32),
            pltpu.VMEM((bits,) + shape, jnp.float32),
            pltpu.VMEM(shape, jnp.float32),
            DMA((depth - 1,)),
            DMA((depth - 1,)),
            DMA((bits,)),
            DMA((bits,)),
            DMA((1,)),
            DMA((1,)),
        ]

    def start(self):
        place = self.place
        for k in range(1, place.depth):
            target = place.at(place.blk, lax.rem(place.z + k, place.depth), place.core)
            send(self.stages.at[0], self.from_z.at[k - 1], self.z_s.at[k - 1], self.z_r.at[k - 1], target)

    def step(self, n):
        place = self.place
        if n == 0:
            value = self.stages[0]
            for k in range(1, place.depth):
                arrived(self.from_z.at[k - 1], self.z_r.at[k - 1])
                value = value + self.from_z[k - 1]
        else:
            arrived(self.from_blk.at[n - 1], self.b_r.at[n - 1])
            value = self.stages[n] + self.from_blk[n - 1]
        self.stages[n + 1] = value
        if n < place.bits:
            target = place.at(place.blk ^ (1 << n), place.z, place.core)
            send(self.stages.at[n + 1], self.from_blk.at[n], self.b_s.at[n], self.b_r.at[n], target)
        else:
            send(self.stages.at[n + 1], self.from_core, self.c_s.at[0], self.c_r.at[0], place.sibling())

    def finish(self):
        place = self.place
        arrived(self.from_core, self.c_r.at[0])
        value = self.stages[place.bits + 1] + self.from_core[...]
        arrived(self.from_core, self.c_s.at[0])
        for n in range(place.bits):
            arrived(self.from_core, self.b_s.at[n])
        for k in range(1, place.depth):
            arrived(self.from_core, self.z_s.at[k - 1])
        return value


class Gather:
    def __init__(self, place, shard, full, sems, only=None):
        self.place, self.shard, self.full, self.only = place, shard, full, only
        self.z_s, self.z_r, self.b_s, self.b_r, self.c_s, self.c_r, self.loc = sems

    @staticmethod
    def sems(sizes):
        blocks, lanes, _ = sizes
        depth = lanes // 2
        return [
            DMA((depth,)),
            DMA((depth,)),
            DMA((depth, blocks - 1)),
            DMA((depth, blocks - 1)),
            DMA((depth,)),
            DMA((depth,)),
            DMA((1 + depth,)),
        ]

    def level(self, k):
        return lax.rem(self.place.z + self.place.depth - k, self.place.depth)

    def chunk(self, blk, k):
        return self.full.at[blk, self.level(k), self.place.core]

    def start(self):
        place = self.place
        for k in range(1, place.depth):
            target = place.at(place.blk, lax.rem(place.z + k, place.depth), place.core)
            send(self.shard, self.chunk(place.blk, 0), self.z_s.at[k], self.z_r.at[k], target)

    def keep(self):
        pltpu.make_async_copy(self.shard, self.chunk(self.place.blk, 0), self.loc.at[0]).start()

    def forward(self, k, t):
        place = self.place
        bit, masks, seen = place.widen(k)[t]
        for n, m in enumerate(masks):
            there = self.chunk(place.blk ^ m, k)
            src = self.shard if m == 0 and k == 0 else there
            send(src, there, self.b_s.at[k, seen + n], self.b_r.at[k, seen + n], place.at(place.blk ^ bit, place.z, place.core))

    def climb(self, k):
        if k > 0:
            arrived(self.chunk(self.place.blk, k), self.z_r.at[k])
        self.forward(k, 0)

    def step(self, k, t):
        place = self.place
        bit, masks, seen = place.widen(k)[t]
        for n, m in enumerate(masks):
            arrived(self.chunk(place.blk ^ bit ^ m, k), self.b_r.at[k, seen + n])
        if t + 1 < place.bits:
            self.forward(k, t + 1)
        else:
            self.swap(k)

    def swap(self, k):
        place = self.place
        if k == 0:
            arrived(self.shard, self.loc.at[0])
        if self.only is None:
            held = self.full.at[:, self.level(k), place.core]
            send(held, held, self.c_s.at[k], self.c_r.at[k], place.sibling())
        else:
            there = self.only.at[:, self.level(k), place.core]
            send(self.full.at[:, self.level(k), place.core, place.other], there, self.c_s.at[k], self.c_r.at[k], place.sibling())
            mine = self.full.at[:, self.level(k), place.core, place.part]
            pltpu.make_async_copy(mine, there, self.loc.at[1 + k]).start()

    def wait_swap(self, k):
        place = self.place
        if self.only is None:
            arrived(self.full.at[:, self.level(k), 1 - place.core], self.c_r.at[k])
        else:
            arrived(self.only.at[:, self.level(k), 1 - place.core], self.c_r.at[k])
            arrived(self.only.at[:, self.level(k), place.core], self.loc.at[1 + k])

    def finish(self):
        place = self.place
        for k in range(place.depth):
            if self.only is None:
                self.wait_swap(k)
                arrived(self.full.at[:, 0, 0], self.c_s.at[k])
            else:
                arrived(self.only.at[:, 0, 0], self.c_s.at[k])
            if k > 0:
                arrived(self.shard, self.z_s.at[k])
            for n in range(place.blocks - 1):
                arrived(self.shard, self.b_s.at[k, n])


class GatherAcross(Gather):
    def start(self):
        place = self.place
        for m in range(1, place.blocks):
            target = place.at(place.blk ^ m, place.z, place.core)
            send(self.shard, self.chunk(place.blk, 0), self.b_s.at[0, m - 1], self.b_r.at[0, m - 1], target)

    def climb(self):
        place = self.place
        for m in range(1, place.blocks):
            arrived(self.chunk(place.blk ^ m, 0), self.b_r.at[0, m - 1])
        arrived(self.shard, self.loc.at[0])
        held = self.full.at[:, place.z, place.core]
        for k in range(1, place.depth):
            target = place.at(place.blk, lax.rem(place.z + k, place.depth), place.core)
            send(held, held, self.z_s.at[k], self.z_r.at[k], target)
        self.pass_on(0)

    def pass_on(self, k):
        held = self.full.at[:, self.level(k), self.place.core]
        if k > 0:
            arrived(held, self.z_r.at[k])
        send(held, held, self.c_s.at[k], self.c_r.at[k], self.place.sibling())

    def finish(self):
        place = self.place
        for k in range(place.depth):
            self.wait_swap(k)
            arrived(self.full.at[:, 0, 0], self.c_s.at[k])
            if k > 0:
                arrived(self.full.at[:, 0, 0], self.z_s.at[k])
        for m in range(1, place.blocks):
            arrived(self.shard, self.b_s.at[0, m - 1])


def first_kernel(sizes, block, pairs, *refs):
    place = Place(*sizes)
    tok, vec, w_qkv, w_out, w_up, w_down = refs[:6]
    att_ref, lse_ref, tok_own, normed_out, qkv_out, cols_out, vec_out, stage, out_full, up_full, down_full = refs[6:17]
    tok_v, norm_v, norm_t, chunk_v, w32_v, cols_v, qkv_v, kh, vt, run_m, run_l, run_a = refs[17:29]
    tok_s, tok_r, near_s, near_r, loc = refs[29:34]
    total = Total(place, *refs[34:38], refs[38:44])
    qkv = Gather(place, w_qkv, stage, refs[44:51], chunk_v)
    outw = Gather(place, w_out, out_full, refs[51:58])
    upw = Gather(place, w_up, up_full, refs[58:65])
    downw = GatherAcross(place, w_down, down_full, refs[65:72])
    blocks, depth, seqs, share, bits = place.blocks, place.depth, place.seqs, place.share, place.bits
    blk, z, core, home = place.blk, place.z, place.core, place.home
    pair = pl.program_id(0)
    rows, model = tok_v.shape[1:]
    length = blocks * rows
    count = length // block
    owned = w_qkv.shape[1]
    per_seq = share // 2
    local = lambda src, dst, sem: pltpu.make_async_copy(src, dst, sem).start()

    @pl.when(pair == 0)
    def _():
        total.stages[0] = vec[...]
        greet(place.peers(True, True))
        total.start()
        qkv.start()
        for i in range(seqs):
            for h in range(per_seq):
                target = (core * seqs + i) * per_seq + h

                @pl.when(target != blk)
                def _(i=i, h=h, target=target):
                    sems = tok_s.at[i * per_seq + h], tok_r.at[blk]
                    send(tok.at[i], tok_v.at[blk], *sems, place.at(target, z, core))

                @pl.when(target == blk)
                def _(i=i):
                    local(tok.at[i], tok_v.at[blk], loc.at[0])

        qkv.forward(0, 0)
        for array in (qkv, outw, upw, downw):
            array.keep()
        for k in range(1, depth):
            qkv.climb(k)
        outw.start()
        upw.start()
        total.step(0)
        total.step(1)

        @pl.when(core == home)
        def _():
            for p in range(blocks):

                @pl.when(p != blk)
                def _():
                    arrived(tok_v.at[p], tok_r.at[p])

                @pl.when(p == blk)
                def _():
                    arrived(tok_v.at[p], loc.at[0])

                send(tok_v.at[p], tok_v.at[p], near_s.at[p], near_r.at[p], place.sibling())

        for n in range(2, bits + 1):
            total.step(n)
        for t in range(bits):
            for k in range(depth):
                qkv.step(k, t)
            if t == 0:
                downw.start()
        for array in (outw, upw):
            for k in range(depth):
                array.climb(k)
        vec_out[...] = total.finish()
        gain, shift = vec_out[0:1, :], vec_out[1:2, :]
        part_rows = min(rows, 128)

        for p in range(blocks):

            @pl.when(core != home)
            def _(p=p):
                arrived(tok_v.at[p], near_r.at[p])

            def norm(i, _, p=p):
                inside = pl.ds(pl.multiple_of(i * part_rows, part_rows), part_rows)
                unit, _ = centered(tok_v[p, inside, :].astype(jnp.float32))
                at = pl.ds(pl.multiple_of(p * rows + i * part_rows, part_rows), part_rows)
                normed = unit * gain + shift
                norm_v[at, :] = normed.astype(jnp.bfloat16)
                norm_t[:, at] = normed.T.astype(jnp.bfloat16)
                return 0

            lax.fori_loop(0, rows // part_rows, norm, 0)
        local(norm_t, normed_out, loc.at[1])
        for t in range(place.per_part):
            local(tok_v.at[place.part * place.per_part + t], tok_own.at[t], loc.at[2 + t])
        downw.climb()
        for k in range(depth):
            qkv.wait_swap(k)
        for b in range(blocks):
            for d in range(depth):
                for c in range(2):
                    index = (b * depth + d) * 2 + c
                    w32_v[index * owned : (index + 1) * owned, :] = chunk_v[b, d, c].astype(jnp.float32)
        cols_v[...] = w32_v[...].astype(jnp.bfloat16)
        local(cols_v, cols_out, loc.at[2 + place.per_part])

        def project(i, _):
            at = pl.ds(pl.multiple_of(i * block, block), block)
            normed = norm_v[at, :]
            scale = jnp.where(lax.broadcasted_iota(jnp.int32, (1, 384), 1) < 128, 0.125, 1.0)
            for n in range(pairs):
                value = dot_nn(normed, cols_v[:, n * 384 : (n + 1) * 384]) * scale
                qkv_v[at, n * 384 : (n + 1) * 384] = value.astype(jnp.bfloat16)
            return 0

        lax.fori_loop(0, count, project, 0)
        local(qkv_v, qkv_out, loc.at[3 + place.per_part])

    per_pair = count * (count + 1) // 2
    tasks = []
    levels = [(array, k) for array in (outw, upw) for k in range(depth)]
    for n, (array, k) in enumerate(levels):
        for t in range(bits):
            where = 0.3 * t + (0.05 + 0.15 * t) * n / len(levels)
            tasks.append((where, functools.partial(array.step, k, t)))
    for k in range(1, depth):
        tasks.append((0.6 + 0.25 * k / depth, functools.partial(downw.pass_on, k)))
    tasks.sort(key=lambda task: task[0])
    todo = plan(tasks, pairs * per_pair)

    def lanes_of(n):
        return pl.ds(pl.multiple_of(pair * 384 + n * 128, 128), 128)

    split_heads(kh, qkv_v[:, lanes_of(1)])
    vt[...] = qkv_v[:, lanes_of(2)].astype(jnp.float32).T.astype(jnp.bfloat16)

    def q_step(qi, _):
        at_q = pl.ds(pl.multiple_of(qi * block, block), block)
        run_m[...] = jnp.full_like(run_m, -1e30)
        run_l[...] = jnp.zeros_like(run_l)
        run_a[...] = jnp.zeros_like(run_a)

        def one(kj, masked):
            at = pl.ds(pl.multiple_of(kj * block, block), block)
            q_rows = qkv_v[at_q, lanes_of(0)]
            for h in range(2):
                peak, so_far = run_m[h : h + 1, :], run_l[h : h + 1, :]
                s = dot_nt(kh[h, at, :], q_rows)
                u = s * s + 1.0
                inv = lax.rsqrt(u)
                mag = u * inv
                if masked:
                    mag = jnp.where(causal(block, block, kj, qi), mag, -1e30)
                new = jnp.maximum(peak, jnp.max(mag, axis=0, keepdims=True))
                p = jnp.exp(mag - new)
                alpha = jnp.exp(peak - new)
                run_m[h : h + 1, :] = new
                run_l[h : h + 1, :] = so_far * alpha + jnp.sum(p, axis=0, keepdims=True)
                signed = (p * (s * inv)).astype(jnp.bfloat16)
                head = slice(64 * h, 64 * h + 64)
                run_a[head, :] = run_a[head, :] * alpha + dot_nn(vt[head, at], signed)

        def k_step(kj, _):
            @pl.when(kj == qi)
            def _():
                one(kj, True)

            @pl.when(kj != qi)
            def _():
                one(kj, False)

            pump(todo, pair * per_pair + qi * (qi + 1) // 2 + kj)
            return 0

        lax.fori_loop(0, qi + 1, k_step, 0)
        both = []
        for h in range(2):
            both.append(run_a[64 * h : 64 * h + 64, :] / run_l[h : h + 1, :])
            lse_ref[0, h : h + 1, at_q] = run_m[h : h + 1, :] + jnp.log(run_l[h : h + 1, :])
        att_ref[at_q, :] = jnp.concatenate(both, 0).T.astype(jnp.bfloat16)
        return 0

    lax.fori_loop(0, count, q_step, 0)

    @pl.when(pair == pairs - 1)
    def _():
        for array in (qkv, outw, upw, downw):
            array.finish()
        arrived(norm_t, loc.at[1])
        arrived(cols_v, loc.at[2 + place.per_part])
        arrived(qkv_v, loc.at[3 + place.per_part])
        for t in range(place.per_part):
            arrived(tok_own.at[t], loc.at[2 + t])

        @pl.when(core == home)
        def _():
            for p in range(blocks):
                arrived(tok_v.at[p], near_s.at[p])

        for i in range(seqs):
            for h in range(per_seq):
                target = (core * seqs + i) * per_seq + h

                @pl.when(target != blk)
                def _(i=i, h=h):
                    arrived(tok.at[i], tok_s.at[i * per_seq + h])

                @pl.when((target == blk) & (core != home))
                def _():
                    arrived(tok_v.at[blk], loc.at[0])


def first_half(sizes, tok, vec, w_qkv, w_out, w_up, w_down, block):
    blocks, lanes, seqs = sizes
    depth, share = lanes // 2, blocks // seqs
    per_part = blocks // share
    rows, model = tok.shape[1:]
    length = blocks * rows
    width = w_qkv.shape[2]
    pairs = width // 384
    low, full = jnp.bfloat16, jnp.float32
    shape = jax.ShapeDtypeStruct
    owners = (blocks, depth, 2)
    in_vmem = pl.BlockSpec(memory_space=pltpu.VMEM)
    return pl.pallas_call(
        functools.partial(first_kernel, sizes, block, pairs),
        grid=(pairs,),
        out_shape=[
            shape((length, 128 * pairs), low),
            shape((pairs, 8, length), full),
            shape((per_part, rows, model), low),
            shape((model, length), low),
            shape((length, width), low),
            shape((model, width), low),
            shape(vec.shape, full),
            shape(owners + w_qkv.shape, low),
            shape(owners + w_out.shape, low),
            shape(owners + w_up.shape, low),
            shape(owners + w_down.shape, low),
        ],
        in_specs=[ANYWHERE, in_vmem] + [ANYWHERE] * 4,
        out_specs=[pl.BlockSpec((length, 128), lambda p: (0, p)), pl.BlockSpec((1, 8, length), lambda p: (p, 0, 0))]
        + [ANYWHERE] * 4
        + [in_vmem]
        + [ANYWHERE] * 4,
        scratch_shapes=[
            pltpu.VMEM((blocks, rows, model), low),
            pltpu.VMEM((length, model), low),
            pltpu.VMEM((model, length), low),
            pltpu.VMEM(owners + w_qkv.shape[1:], low),
            pltpu.VMEM((model, width), full),
            pltpu.VMEM((model, width), low),
            pltpu.VMEM((length, width), low),
            pltpu.VMEM((2, length, 128), low),
            pltpu.VMEM((128, length), low),
            pltpu.VMEM((8, block), full),
            pltpu.VMEM((8, block), full),
            pltpu.VMEM((128, block), full),
            DMA((seqs * share // 2,)),
            DMA((blocks,)),
            DMA((blocks,)),
            DMA((blocks,)),
            DMA((4 + per_part,)),
        ]
        + Total.scratch(sizes, vec.shape)
        + Gather.sems(sizes) * 4,
        compiler_params=pltpu.CompilerParams(collective_id=0, has_side_effects=True, vmem_limit_bytes=VMEM_LIMIT),
    )(tok, vec, w_qkv, w_out, w_up, w_down)


def dot_tn(left, right):
    return lax.dot_general(left, right, (((0,), (0,)), ((), ())), preferred_element_type=jnp.float32)


def centered(values):
    center = jnp.mean(values, axis=-1, keepdims=True)
    offsets = values - center
    spread = jnp.mean(offsets * offsets, axis=-1, keepdims=True)
    inverse = lax.rsqrt(spread + 1e-05)
    return offsets * inverse, inverse


def norm_back(values, grads, gain):
    unit, inverse = centered(values)
    scaled = grads * gain
    first = jnp.mean(scaled, axis=-1, keepdims=True)
    second = jnp.mean(scaled * unit, axis=-1, keepdims=True)
    back = inverse * (scaled - first - unit * second)
    return back, jnp.sum(grads * unit, axis=0, keepdims=True), jnp.sum(grads, axis=0, keepdims=True)


def gelu_parts(x):
    square = x * x
    half = 0.5 + 0.5 * jnp.tanh(0.7978845608028654 * x * (1.0 + 0.044715 * square))
    slope = half + x * (2.0 * half * (1.0 - half)) * (0.7978845608028654 + 0.1070322243 * square)
    return x * half, slope


def mlp_kernel(sizes, cols, tile, chunk, *refs):
    place = Place(*sizes)
    att, tok_own, cot, w_out, w_up, w_down, vec, live = refs[:8]
    result, g_heads, g_mid, g_out, g_up, g_down, g_vec = refs[8:15]
    (att_v, tok_v, cot_v, res_v, out_v, up_v, down_v, mid_v, n2_v, n2t_v, hid_v, slope_v, sum_v, ga_v) = refs[15:29]
    (st_out, st_up, st_down) = refs[29:32]
    a_s, a_r, g_s, g_r, cot_s, cot_r, m_s, m_r, loc, up_l, down_l, o_l = refs[32:]
    share, per_part, seqs = place.share, place.per_part, place.seqs
    part, blk, z, core = place.part, place.blk, place.z, place.core
    rows, model = mid_v.shape
    block = rows // per_part
    ff = up_v.shape[1]
    chunks, tiles = ff // chunk, rows // tile
    flat = blk * 2 + core
    partners = [((flat ^ k) // 2, z, (flat ^ k) % 2) for k in range(1, share)]
    slot_of = lax.rem(place.seq, seqs)
    greet(place.peers(False, True))
    for k in range(1, share):
        send(att.at[part ^ k], att_v.at[part], a_s.at[k - 1], a_r.at[k - 1], place.at(*partners[k - 1]))

    def local(src, dst, sem):
        pltpu.make_async_copy(src, dst, sem).start()

    local(att.at[part], att_v.at[part], loc.at[0])
    for t in range(per_part):
        local(tok_own.at[t], tok_v.at[t], loc.at[1 + t])
    local(w_out, out_v, loc.at[1 + per_part])
    for i in range(seqs):
        owner = (core * seqs + i) * share + blk // per_part
        slot = lax.rem(blk, per_part)

        @pl.when(owner != flat)
        def _(i=i, owner=owner, slot=slot):
            send(cot.at[i], cot_v.at[slot], cot_s.at[i], cot_r.at[slot], place.at(owner // 2, z, owner % 2))

        @pl.when(owner == flat)
        def _(i=i, slot=slot):
            local(cot.at[i], cot_v.at[slot], loc.at[2 + per_part])

    def span(f):
        return pl.ds(pl.multiple_of(f * chunk, chunk), chunk)

    for f in range(chunks):
        local(w_up.at[:, pl.ds(f * chunk, chunk)], up_v.at[:, pl.ds(f * chunk, chunk)], up_l.at[f])
        local(w_down.at[pl.ds(f * chunk, chunk)], down_v.at[pl.ds(f * chunk, chunk)], down_l.at[f])

    arrived(att_v.at[part], loc.at[0])
    for t in range(per_part):
        arrived(tok_v.at[t], loc.at[1 + t])
    arrived(out_v, loc.at[1 + per_part])
    for k in range(1, share):
        arrived(att_v.at[part ^ k], a_r.at[k - 1])
    gain, shift = vec[2:3, :], vec[3:4, :]
    per_block = block // tile

    def spot(i):
        return i // per_block, pl.ds(pl.multiple_of(lax.rem(i, per_block) * tile, tile), tile)

    def enter(i, _):
        at = pl.ds(pl.multiple_of(i * tile, tile), tile)
        branch = dot_nn(att_v[0, at, :cols], out_v[:cols, :])
        for g in range(1, share):
            branch = branch + dot_nn(att_v[g, at, :cols], out_v[g * cols : (g + 1) * cols, :])
        t, inside = spot(i)
        middle = tok_v[t, inside, :].astype(jnp.float32) + live[at, :] * branch
        mid_v[at, :] = middle
        unit, _ = centered(middle)
        normed = unit * gain + shift
        n2_v[at, :] = normed.astype(jnp.bfloat16)
        n2t_v[:, at] = normed.T.astype(jnp.bfloat16)
        return 0

    lax.fori_loop(0, tiles, enter, 0)
    sum_v[...] = mid_v[...]

    def up_step(f, _):
        arrived(up_v.at[:, span(f)], up_l.at[f])
        arrived(down_v.at[span(f)], down_l.at[f])
        hidden, slope = gelu_parts(dot_nn(n2_v[...], up_v[:, span(f)]))
        hidden = hidden.astype(jnp.bfloat16)
        hid_v[:, span(f)] = hidden
        slope_v[:, span(f)] = slope.astype(jnp.bfloat16)
        sum_v[...] += dot_nn(hidden, down_v[span(f), :])
        return 0

    lax.fori_loop(0, chunks, up_step, 0)
    for t in range(per_part):
        res_v[t] = sum_v[t * block : (t + 1) * block, :].astype(jnp.bfloat16)
        source = part * per_part + t
        mine = (source == blk) & (place.home == core)

        @pl.when(mine)
        def _(t=t):
            local(res_v.at[t], result.at[slot_of], loc.at[0])

        @pl.when(jnp.logical_not(mine))
        def _(t=t, source=source):
            send(res_v.at[t], result.at[slot_of], m_s.at[t], m_r.at[slot_of], place.at(source, z, place.home))

    for t in range(per_part):
        mine = (part * per_part + t == blk) & (place.home == core)

        @pl.when(mine)
        def _(t=t):
            arrived(cot_v.at[t], loc.at[2 + per_part])

        @pl.when(jnp.logical_not(mine))
        def _(t=t):
            arrived(cot_v.at[t], cot_r.at[t])

    sum_v[...] = jnp.zeros_like(sum_v)

    def back_step(f, _):
        top = cot_v[...].reshape(rows, model)
        grad_pre = (dot_nt(top, down_v[span(f), :]) * slope_v[:, span(f)].astype(jnp.float32)).astype(jnp.bfloat16)
        now = lax.rem(f, 2)

        @pl.when(f >= 2)
        def _():
            arrived(st_down.at[now], o_l.at[now])
            arrived(st_up.at[now], o_l.at[2 + now])

        st_down[now] = dot_tn(hid_v[:, span(f)], top).astype(jnp.bfloat16)
        st_up[now] = dot_nn(n2t_v[...], grad_pre).astype(jnp.bfloat16)
        local(st_down.at[now], g_down.at[span(f)], o_l.at[now])
        local(st_up.at[now], g_up.at[:, span(f)], o_l.at[2 + now])
        sum_v[...] += dot_nt(grad_pre, up_v[:, span(f)])
        return 0

    lax.fori_loop(0, chunks, back_step, 0)
    g_vec[...] = jnp.zeros_like(g_vec)

    def leave(i, _):
        at = pl.ds(pl.multiple_of(i * tile, tile), tile)
        t, inside = spot(i)
        back, d_gain, d_shift = norm_back(mid_v[at, :], sum_v[at, :], gain)
        g_vec[0:1, :] += d_gain
        g_vec[1:2, :] += d_shift
        total = cot_v[t, inside, :].astype(jnp.float32) + back
        mid_v[at, :] = total
        branch = (live[at, :] * total).astype(jnp.bfloat16)
        n2_v[at, :] = branch
        heads = dot_nt(branch, out_v[...]).astype(jnp.bfloat16)
        for g in range(share):
            if cols == ga_v.shape[2]:
                ga_v[g, at, :] = heads[:, g * cols : (g + 1) * cols]
            else:
                piece = heads[:, g * cols : (g + 1) * cols]
                ga_v[g, at, :] = jnp.concatenate([piece, jnp.zeros((tile, ga_v.shape[2] - cols), jnp.bfloat16)], 1)
        return 0

    lax.fori_loop(0, tiles, leave, 0)
    for k in range(1, share):
        send(ga_v.at[part ^ k], g_heads.at[part], g_s.at[k - 1], g_r.at[k - 1], place.at(*partners[k - 1]))
    local(ga_v.at[part], g_heads.at[part], loc.at[1])
    local(mid_v, g_mid, loc.at[2])
    for g in range(share):
        st_out[g * cols : (g + 1) * cols, :] = dot_tn(att_v[g, :, :cols], n2_v[...]).astype(jnp.bfloat16)
    local(st_out, g_out, loc.at[1 + per_part])
    for n in range(min(2, chunks)):
        arrived(st_down.at[n], o_l.at[n])
        arrived(st_up.at[n], o_l.at[2 + n])
    arrived(st_out, loc.at[1 + per_part])
    arrived(mid_v, loc.at[2])
    arrived(ga_v.at[part], loc.at[1])
    for k in range(1, share):
        arrived(att.at[part ^ k], a_s.at[k - 1])
        arrived(ga_v.at[part ^ k], g_s.at[k - 1])
        arrived(g_heads.at[part ^ k], g_r.at[k - 1])
    for i in range(seqs):
        owner = (core * seqs + i) * share + blk // per_part

        @pl.when(owner != flat)
        def _(i=i):
            arrived(cot.at[i], cot_s.at[i])
            arrived(result.at[i], m_r.at[i])

    for t in range(per_part):
        mine = (part * per_part + t == blk) & (place.home == core)

        @pl.when(mine)
        def _(t=t):
            arrived(res_v.at[t], loc.at[0])

        @pl.when(jnp.logical_not(mine))
        def _(t=t):
            arrived(res_v.at[t], m_s.at[t])


def feed_forward(sizes, cols, att, tok_own, cot, w_out, w_up, w_down, vec, live, tile, chunk):
    blocks, lanes, seqs = sizes
    share = blocks // seqs
    per_part = blocks // share
    block, model = tok_own.shape[1:]
    rows = per_part * block
    wide = att.shape[2]
    ff = w_up.shape[1]
    chunks = ff // chunk
    in_vmem = pl.BlockSpec(memory_space=pltpu.VMEM)
    low, full = jnp.bfloat16, jnp.float32
    return pl.pallas_call(
        functools.partial(mlp_kernel, sizes, cols, tile, chunk),
        out_shape=[
            jax.ShapeDtypeStruct((seqs, block, model), low),
            jax.ShapeDtypeStruct((share, rows, wide), low),
            jax.ShapeDtypeStruct((rows, model), full),
            jax.ShapeDtypeStruct((model, model), low),
            jax.ShapeDtypeStruct((model, ff), low),
            jax.ShapeDtypeStruct((ff, model), low),
            jax.ShapeDtypeStruct((8, model), full),
        ],
        in_specs=[ANYWHERE] * 6 + [in_vmem] * 2,
        out_specs=[ANYWHERE] * 6 + [in_vmem],
        scratch_shapes=[
            pltpu.VMEM((share, rows, wide), low),
            pltpu.VMEM((per_part, block, model), low),
            pltpu.VMEM((per_part, block, model), low),
            pltpu.VMEM((per_part, block, model), low),
            pltpu.VMEM((model, model), low),
            pltpu.VMEM((model, ff), low),
            pltpu.VMEM((ff, model), low),
            pltpu.VMEM((rows, model), full),
            pltpu.VMEM((rows, model), low),
            pltpu.VMEM((model, rows), low),
            pltpu.VMEM((rows, ff), low),
            pltpu.VMEM((rows, ff), low),
            pltpu.VMEM((rows, model), full),
            pltpu.VMEM((share, rows, wide), low),
            pltpu.VMEM((model, model), low),
            pltpu.VMEM((2, model, chunk), low),
            pltpu.VMEM((2, chunk, model), low),
            DMA((share,)),
            DMA((share,)),
            DMA((share,)),
            DMA((share,)),
            DMA((seqs,)),
            DMA((per_part,)),
            DMA((per_part,)),
            DMA((seqs,)),
            DMA((3 + per_part,)),
            DMA((chunks,)),
            DMA((chunks,)),
            DMA((4,)),
        ],
        compiler_params=pltpu.CompilerParams(collective_id=4, has_side_effects=True, vmem_limit_bytes=VMEM_LIMIT),
    )(att, tok_own, cot, w_out, w_up, w_down, vec, live)


def last_kernel(sizes, block, pairs, *refs):
    place = Place(*sizes)
    blocks, depth, seqs, share, bits = place.blocks, place.depth, place.seqs, place.share, place.bits
    blk, z, core, part = place.blk, place.z, place.core, place.part
    per_part = place.per_part
    count = 3 + pairs
    q_ref, k_ref, v_ref, g_ref, att_ref, lse_ref = refs[:6]
    big, tok_own, g_mid, norm_t, cols, vec, two = refs[6:9], refs[9], refs[10], refs[11], refs[12], refs[13], refs[14]
    refs = refs[15:]
    sums, tok_out, vec_out, refs = refs[:count], refs[count], refs[count + 1], refs[count + 2 :]
    kh, vh, qh, gh, kt, delta, dqt, dk, dv = refs[:9]
    gq_v, own_v, norm_v, cols_v, tok_v, mid_v, out_v, part_v, got_v, sum_v = refs[9:19]
    p_s, p_r, t_s, t_r, loc = refs[19:24]
    total = Total(place, *refs[24:28], refs[28:34])
    kinds = ["rows"] * 3 + ["columns"] * pairs
    fold = Fold(place, kinds, list(big) + [own_v.at[p] for p in range(pairs)], [], sums, [], refs[34:])
    pair = pl.program_id(0)
    length = q_ref.shape[0]
    rows, model = mid_v.shape
    owned = own_v.shape[4]
    steps = length // block
    per_pair = steps * (steps + 1) // 2
    flat = blk * 2 + core
    partners = [((flat ^ k) // 2, z, (flat ^ k) % 2) for k in range(1, share)]
    slot_of = lax.rem(place.seq, seqs)
    local = lambda src, dst, sem: pltpu.make_async_copy(src, dst, sem).start()

    tasks = []
    units = [(a, k) for a in range(3) for k in fold.order]
    scale = 12.0 / len(units) / 80.0
    for n, (a, k) in enumerate(units):
        tasks.append(((3 + 1.3 * n) * scale, functools.partial(fold.join, a, k)))
        for t in range(bits):
            where = 8 + 6 * t + (3.2 + 0.4 * t) * n
            tasks.append((where * scale, functools.partial(fold.step, a, k, t)))
    for a in range(3):
        tasks.append((0.78 + 0.05 * a, functools.partial(fold.total, a)))
    for p in range(pairs - 1):
        for n, k in enumerate(fold.order):
            tasks.append(((p + 1.15) / pairs, functools.partial(fold.join, 3 + p, k)))
            for t in range(bits):
                where = p + 1.4 + 0.5 * t / bits + 0.1 * n / depth
                tasks.append((where / pairs, functools.partial(fold.step, 3 + p, k, t)))
    tasks.sort(key=lambda task: task[0])
    todo = plan(tasks, pairs * per_pair)

    @pl.when(pair == 0)
    def _():
        fold.greet()
        fold.clear()
        for a, k in units:
            fold.start(a, k)
        local(norm_t, norm_v, loc.at[0])
        local(cols, cols_v, loc.at[1])
        local(g_mid, mid_v, loc.at[2])
        local(tok_own, tok_v, loc.at[3])

    split_heads(kh, k_ref[...])
    split_heads(vh, v_ref[...])
    split_heads(qh, q_ref[...])
    split_heads(gh, g_ref[...])
    kt[...] = k_ref[...].astype(jnp.float32).T.astype(jnp.bfloat16)
    prod = (g_ref[...].astype(jnp.float32) * att_ref[...].astype(jnp.float32)).T
    delta[0:1, :] = jnp.sum(prod[:64], axis=0, keepdims=True)
    delta[1:2, :] = jnp.sum(prod[64:], axis=0, keepdims=True)
    dqt[...] = jnp.zeros_like(dqt)

    def k_step(kj, _):
        at = pl.ds(pl.multiple_of(kj * block, block), block)

        def one(qi, masked):
            at_q = pl.ds(pl.multiple_of(qi * block, block), block)
            q_rows = q_ref[at_q, :]
            g_rows = g_ref[at_q, :]
            add_k = add_v = None
            for h in range(2):
                s = dot_nt(kh[h, at, :], q_rows)
                dp = dot_nt(vh[h, at, :], g_rows)
                u = s * s + 1.0
                inv = lax.rsqrt(u)
                arg = u * inv - lse_ref[0, h : h + 1, at_q]
                if masked:
                    arg = jnp.where(causal(block, block, kj, qi), arg, -1e30)
                p = jnp.exp(arg)
                sgn = s * inv
                t = inv * inv * (inv - 1.0) + 1.0
                ds = (p * (dp * t - sgn * delta[h : h + 1, at_q])).astype(jnp.bfloat16)
                signed = (p * sgn).astype(jnp.bfloat16)
                one_v = dot_nn(signed, gh[h, at_q, :])
                one_k = dot_nn(ds, qh[h, at_q, :])
                add_v = one_v if h == 0 else add_v + one_v
                add_k = one_k if h == 0 else add_k + one_k
                dqt[64 * h : 64 * h + 64, at_q] += dot_nn(kt[64 * h : 64 * h + 64, at], ds)
            return add_k, add_v

        def more(qi, _):
            @pl.when(qi == kj)
            def _():
                dk[...], dv[...] = one(qi, True)

            @pl.when(qi != kj)
            def _():
                add_k, add_v = one(qi, False)
                dk[...] += add_k
                dv[...] += add_v

            pump(todo, pair * per_pair + kj * steps - kj * (kj - 1) // 2 + qi - kj)
            return 0

        lax.fori_loop(kj, steps, more, 0)
        gq_v[pair, at, 128:256] = dk[...].astype(jnp.bfloat16)
        gq_v[pair, at, 256:384] = dv[...].astype(jnp.bfloat16)
        return 0

    lax.fori_loop(0, steps, k_step, 0)
    gq_v[pair, :, 0:128] = (dqt[...] * 0.125).T.astype(jnp.bfloat16)

    @pl.when(pair == 0)
    def _():
        arrived(norm_v, loc.at[0])
        arrived(cols_v, loc.at[1])
        arrived(mid_v, loc.at[2])
        arrived(tok_v, loc.at[3])

    sum_v[...] = dot_nn(norm_v[...], gq_v[pair])
    for b in range(blocks):
        for d in range(depth):
            for c in range(2):
                first = ((b * depth + d) * 2 + c) * owned
                own_v[pair, b, d, c] = sum_v[first : first + owned, :].astype(jnp.bfloat16)
    for p in range(pairs):

        @pl.when(pair == p)
        def _(p=p):
            for k in fold.order:
                fold.start(3 + p, k)

    @pl.when(pair == pairs - 1)
    def _():
        mine = 3 + pairs - 1
        tile = min(256, block, rows)

        def input_grad(g, i):
            at = pl.ds(pl.multiple_of(g * rows + i * tile, tile), tile)
            value = dot_nt(gq_v[0, at, :], cols_v[:, 0:384])
            for p in range(1, pairs):
                value = value + dot_nt(gq_v[p, at, :], cols_v[:, p * 384 : (p + 1) * 384])
            return value

        for k in range(1, share):

            def away(i, _, k=k):
                at = pl.ds(pl.multiple_of(i * tile, tile), tile)
                part_v[k - 1, at, :] = input_grad(part ^ k, i).astype(jnp.bfloat16)
                return 0

            lax.fori_loop(0, rows // tile, away, 0)
            send(part_v.at[k - 1], got_v.at[k - 1], p_s.at[k - 1], p_r.at[k - 1], place.at(*partners[k - 1]))
        for k in fold.order:
            fold.join(mine, k)
        total.stages[0] = jnp.zeros(total.stages.shape[1:], jnp.float32)
        total.stages[0, 2:4, :] = two[0:2, :]
        gain = vec[0:1, :]
        per_block = rows // per_part // tile

        def leave(i, _):
            at = pl.ds(pl.multiple_of(i * tile, tile), tile)
            t = i // per_block
            inside = pl.ds(pl.multiple_of(lax.rem(i, per_block) * tile, tile), tile)
            value = input_grad(part, i)
            for k in range(1, share):
                value = value + got_v[k - 1, at, :].astype(jnp.float32)
            back, d_gain, d_shift = norm_back(tok_v[t, inside, :].astype(jnp.float32), value, gain)
            total.stages[0, 0:1, :] += d_gain
            total.stages[0, 1:2, :] += d_shift
            out_v[t, inside, :] = (mid_v[at, :] + back).astype(jnp.bfloat16)
            return 0

        for k in range(1, share):
            arrived(got_v.at[k - 1], p_r.at[k - 1])
        for t in range(per_part):
            lax.fori_loop(t * per_block, (t + 1) * per_block, leave, 0)
            source = part * per_part + t
            here = (source == blk) & (place.home == core)

            @pl.when(here)
            def _(t=t):
                local(out_v.at[t], tok_out.at[slot_of], loc.at[0])

            @pl.when(jnp.logical_not(here))
            def _(t=t, source=source):
                send(out_v.at[t], tok_out.at[slot_of], t_s.at[t], t_r.at[slot_of], place.at(source, z, place.home))

            if t == 0:
                for k in fold.order:
                    fold.step(mine, k, 0)
        total.start()
        for t in range(1, bits):
            for k in fold.order:
                fold.step(mine, k, t)
        for n in range(bits + 1):
            total.step(n)
        for p in range(pairs):
            fold.total(3 + p)
        vec_out[...] = total.finish()
        fold.finish()
        for k in range(1, share):
            arrived(part_v.at[k - 1], p_s.at[k - 1])
        for t in range(per_part):
            here = (part * per_part + t == blk) & (place.home == core)

            @pl.when(here)
            def _(t=t):
                arrived(out_v.at[t], loc.at[0])

            @pl.when(jnp.logical_not(here))
            def _(t=t):
                arrived(out_v.at[t], t_s.at[t])

        for i in range(seqs):
            owner = (core * seqs + i) * share + blk // per_part

            @pl.when(owner != flat)
            def _(i=i):
                arrived(tok_out.at[i], t_r.at[i])


def last_half(sizes, qkv, g_att, att, lse, big, tok_own, g_mid, norm_t, cols, vec, two, block):
    blocks, lanes, seqs = sizes
    depth, share = lanes // 2, blocks // seqs
    length, width = qkv.shape
    pairs = width // 384
    model = cols.shape[0]
    owned = model // (blocks * lanes)
    per_part, rows_in, _ = tok_own.shape
    rows = per_part * rows_in
    low, full = jnp.bfloat16, jnp.float32
    in_vmem = pl.BlockSpec(memory_space=pltpu.VMEM)
    own = jax.ShapeDtypeStruct((blocks, depth, 2, owned, 384), low)
    kinds = ["rows"] * 3 + ["columns"] * pairs
    out, _, scratch = fold_shapes(sizes, list(big) + [own] * pairs, kinds, [])
    return pl.pallas_call(
        functools.partial(last_kernel, sizes, block, pairs),
        grid=(pairs,),
        out_shape=out + [jax.ShapeDtypeStruct((seqs, rows_in, model), low), jax.ShapeDtypeStruct(vec.shape, full)],
        in_specs=[pl.BlockSpec((length, 128), lambda p, n=n: (0, 3 * p + n)) for n in range(3)]
        + [pl.BlockSpec((length, 128), lambda p: (0, p))] * 2
        + [pl.BlockSpec((1, 8, length), lambda p: (p, 0, 0))]
        + [ANYWHERE] * 7
        + [in_vmem] * 2,
        out_specs=[in_vmem] * len(out) + [ANYWHERE, in_vmem],
        scratch_shapes=[pltpu.VMEM((2, length, 128), low)] * 4
        + [
            pltpu.VMEM((128, length), low),
            pltpu.VMEM((8, length), full),
            pltpu.VMEM((128, length), full),
            pltpu.VMEM((block, 128), full),
            pltpu.VMEM((block, 128), full),
            pltpu.VMEM((pairs, length, 384), low),
            pltpu.VMEM((pairs,) + own.shape, low),
            pltpu.VMEM((model, length), low),
            pltpu.VMEM((model, width), low),
            pltpu.VMEM((per_part, rows_in, model), low),
            pltpu.VMEM((rows, model), full),
            pltpu.VMEM((per_part, rows_in, model), low),
            pltpu.VMEM((share - 1, rows, model), low),
            pltpu.VMEM((share - 1, rows, model), low),
            pltpu.VMEM((model, 384), full),
            DMA((share,)),
            DMA((share,)),
            DMA((per_part,)),
            DMA((seqs,)),
            DMA((4,)),
        ]
        + Total.scratch(sizes, vec.shape)
        + scratch,
        compiler_params=pltpu.CompilerParams(collective_id=2, has_side_effects=True, vmem_limit_bytes=63 * 2**20),
    )(qkv, qkv, qkv, g_att, att, lse, *big, tok_own, g_mid, norm_t, cols, vec, two)


def shards(sizes, tokens, seq_len, ln1_gain, ln1_shift, w_qkv, w_out, ln2_gain, ln2_shift, w_up, w_down, cotangent):
    blocks, lanes, seqs = sizes
    place = Place(*sizes)
    share, part = place.share, place.part
    model = tokens.shape[2]
    length = blocks * tokens.shape[1]
    rows = length // share
    owned = w_qkv.shape[0]
    cols = model // share
    wide = -(-cols // 128) * 128

    pairs = wide // 128
    grouped = jnp.pad(w_qkv.reshape(owned, 3, share, cols), ((0, 0), (0, 0), (0, 0), (0, wide - cols)))
    grouped = grouped.reshape(owned, 3, share, pairs, 128)
    grouped = jnp.transpose(grouped, (2, 0, 3, 1, 4)).reshape(share, owned, 3 * wide)
    flat = place.blk * lanes + lax.axis_index("seq")
    vec = jnp.zeros((8, model), jnp.float32)
    own = jnp.stack([ln1_gain, ln1_shift, ln2_gain, ln2_shift]).astype(jnp.float32)
    vec = lax.dynamic_update_slice(vec, own, (0, flat * owned))
    first = (place.blk == 0).astype(jnp.float32)
    vec = lax.dynamic_update_slice(vec, first * seq_len.astype(jnp.float32)[None], (4, lax.axis_index("seq") * seqs))
    outs = first_half(sizes, tokens, vec, grouped, w_out, w_up, w_down, min(512, rows))
    att, lse, tok_own, norm_t, qkv, qkv_cols, params, _, out_full, up_full, down_full = outs
    out_full, up_full = [a.reshape(model, -1) for a in (out_full, up_full)]
    down_full = down_full.reshape(-1, model)
    my_len = lax.dynamic_index_in_dim(params[4], place.z * 2 * seqs + place.seq, 0, False)

    positions = part * rows + jnp.arange(rows, dtype=jnp.int32)
    live = (positions.astype(jnp.float32) < my_len).astype(jnp.float32)[:, None]
    result, g_heads, grad_mid, grad_out, grad_up, grad_down, two_grads = feed_forward(
        sizes,
        cols,
        att.reshape(share, rows, wide),
        tok_own,
        cotangent,
        out_full,
        up_full,
        down_full,
        params,
        live,
        min(256, tokens.shape[1]),
        min(512, w_up.shape[1]),
    )

    def cut(values):
        return values.reshape((blocks, lanes // 2, 2, -1) + values.shape[1:])

    done = last_half(
        sizes,
        qkv,
        g_heads.reshape(length, wide),
        att,
        lse,
        [cut(grad_out), cut(grad_up), cut(grad_down)],
        tok_own,
        grad_mid,
        norm_t,
        qkv_cols,
        params,
        two_grads,
        min(512, rows),
    )
    sum_out, sum_up, sum_down, *sum_pairs, grad_tokens, vec_sum = done
    vec_own = lax.dynamic_slice_in_dim(vec_sum, flat * owned, owned, 1)
    sum_qkv = jnp.stack(sum_pairs).reshape(pairs, share, owned, 3, 128)
    sum_qkv = jnp.transpose(sum_qkv, (2, 3, 1, 0, 4)).reshape(owned, 3, share, wide)[..., :cols].reshape(owned, 3 * model)
    return (
        result,
        grad_tokens.astype(jnp.float32),
        vec_own[0],
        vec_own[1],
        sum_qkv,
        sum_out,
        vec_own[2],
        vec_own[3],
        sum_up,
        sum_down,
    )


def solution(mesh):
    blocks, lanes = mesh.shape["blk"], mesh.shape["seq"]
    whole = P(("blk", "seq"))
    rows = P(("blk", "seq"), None)
    tokens = P("seq", "blk", None)

    def run(*args):
        seqs = args[0].shape[0] // lanes
        return jax.shard_map(
            functools.partial(shards, (blocks, lanes, seqs)),
            mesh=mesh,
            in_specs=(tokens, P("seq"), whole, whole, rows, rows, whole, whole, rows, rows, tokens),
            out_specs=(tokens, tokens, whole, whole, rows, rows, whole, whole, rows, rows),
            check_vma=False,
        )(*args)

    return run
```

profile of v0, /device:TPU:0, one launch (start us, length us, event | category | flops | bytes accessed | tf_op | source)
XLA Modules:
  0.0 338.4 jit_solution(6472918965446292224)
XLA Ops:
  0.7 0.7 multiply_bitcast_fusion
  1.4 0.7 maximum_convert_fusion
  2.1 0.4 dynamic_update_slice.6
  2.5 0.2 dynamic_update_slice.7.refs_1_
  2.7 1.0 reshape.78
  3.8 0.7 reshape.79.refs_2_
  4.5 123.6 %shard_map.186 = (bf16[2048,384]{1,0:T(8,128)(2,1)}, f32[3,8,2048]{2,1,0:T(8,128)}, bf16[2,512,768]{2,1,0:T(8,128)(2,1)}, bf16[768,2048]{1,0:T(8,128)(2,1)}, bf1...) custom-call(bf16[2,512,768]{2,1,0:T(8,128)(2,1)} %refs_0_.1, ...), custom_call_target="tpu_custom_call" | custom-call | tf_op jit(solution)/shard_map/pallas_call | solution.py:703
  128.1 0.7 slice.15
  128.8 0.6 constant_dynamic-slice_fusion.1
  129.4 1.5 fusion.refs_7_
  130.9 54.8 %shard_map.187 = (bf16[2,512,768]{2,1,0:T(8,128)(2,1)}, bf16[2,1024,384]{2,1,0:T(8,128)(2,1)}, f32[1024,768]{1,0:T(8,128)}, bf16[768,768]{1,0:T(8,128)(2,1)}, bf...) custom-call(bf16[2,1024,384]{2,1,0:T(8,128)(2,1)} %bitcast.26, ...), custom_call_target="tpu_custom_call" | custom-call | tf_op jit(solution)/shard_map/pallas_call | solution.py:977
  185.8 142.2 %shard_map.188 = (f32[24,768]{1,0:T(8,128)}, f32[24,3072]{1,0:T(8,128)}, f32[96,768]{1,0:T(8,128)}, f32[2,24,384]{2,1,0:T(8,128)}, f32[2,24,384]{2,1,0:T(8,128)}...) custom-call(bf16[2048,1152]{1,0:T(8,128)(2,1)} %get-tuple-element.42.refs_0_.refs_1_.refs_2_, ...), custom_call_target="tpu_custom_call" | custom-call | tf_op jit(solution)/shard_map/pallas_call | solution.py:1266
  328.0 0.9 constant_dynamic-slice_fusion
  328.9 0.5 slice_bitcast_fusion
  329.4 0.9 stack.32
  330.3 0.9 stack.33
  331.2 0.9 stack.34
  332.2 0.2 copy.27
  332.4 0.8 reshape_reshape.3
  333.2 1.9 convert_element_type.37
  335.2 1.1 copy.34
  336.3 0.6 copy.35
  336.9 0.7 copy.36
  337.7 0.7 copy.37
  (15 shorter events, 0.2 us)
Async XLA Ops:
  2.7 1.8 copy-start.4
  328.0 5.2 %copy-start.1 = (bf16[2,512,768]{2,1,0:T(8,128)(2,1)S(1)}, bf16[2,512,768]{2,1,0:T(8,128)(2,1)}, u32[]{:S(2)}) copy-start(bf16[2,512,768]{2,1,0:T(8,128)(2,1)} %get-tuple-element.52) | copy-start | bytes 4718596
  333.2 2.0 copy-start
  335.2 1.2 copy-start.5
  335.2 1.8 copy-start.3
  335.2 2.5 copy-start.2
where the time goes:
time: 340 us; the launch traced here: 338 us
  Pallas kernels  321 us (94%)
  local copies, waits for them, and re-layouts  12.1 us (4%)
  other arithmetic  4.87 us (1%)
    pallas_call x1, Pallas kernels, last_half(): pl.pallas_call(functools.partial(last_kernel, sizes, block, pairs), grid=...  142 us
    pallas_call x1, Pallas kernels, first_half(): pl.pallas_call(functools.partial(first_kernel, sizes, block, pairs), grid...  124 us
    pallas_call x1, Pallas kernels, feed_forward(): pl.pallas_call(functools.partial(mlp_kernel, sizes, cols, tile, chunk), o...  54.8 us

commit v1 on v0

--- a/solution.py
+++ b/solution.py
@@ -348,8 +348,10 @@
 
 
 class Gather:
-    def __init__(self, place, shard, full, sems, only=None):
-        self.place, self.shard, self.full, self.only = place, shard, full, only
+    def __init__(self, place, shard, full, sems, only=None, span=None):
+        self.place, self.full, self.only = place, full, only
+        self.tail = () if span is None else (pl.ds(*span),)
+        self.shard = shard if span is None else shard.at[self.tail[0]]
         self.z_s, self.z_r, self.b_s, self.b_r, self.c_s, self.c_r, self.loc = sems
 
     @staticmethod
@@ -369,8 +371,11 @@
     def level(self, k):
         return lax.rem(self.place.z + self.place.depth - k, self.place.depth)
 
+    def lane(self, depth_at, core):
+        return self.full.at[(slice(None), depth_at, core) + self.tail]
+
     def chunk(self, blk, k):
-        return self.full.at[blk, self.level(k), self.place.core]
+        return self.full.at[(blk, self.level(k), self.place.core) + self.tail]
 
     def start(self):
         place = self.place
@@ -409,7 +414,7 @@
         if k == 0:
             arrived(self.shard, self.loc.at[0])
         if self.only is None:
-            held = self.full.at[:, self.level(k), place.core]
+            held = self.lane(self.level(k), place.core)
             send(held, held, self.c_s.at[k], self.c_r.at[k], place.sibling())
         else:
             there = self.only.at[:, self.level(k), place.core]
@@ -420,7 +425,7 @@
     def wait_swap(self, k):
         place = self.place
         if self.only is None:
-            arrived(self.full.at[:, self.level(k), 1 - place.core], self.c_r.at[k])
+            arrived(self.lane(self.level(k), 1 - place.core), self.c_r.at[k])
         else:
             arrived(self.only.at[:, self.level(k), 1 - place.core], self.c_r.at[k])
             arrived(self.only.at[:, self.level(k), place.core], self.loc.at[1 + k])
@@ -430,7 +435,7 @@
         for k in range(place.depth):
             if self.only is None:
                 self.wait_swap(k)
-                arrived(self.full.at[:, 0, 0], self.c_s.at[k])
+                arrived(self.lane(0, 0), self.c_s.at[k])
             else:
                 arrived(self.only.at[:, 0, 0], self.c_s.at[k])
             if k > 0:
@@ -451,14 +456,14 @@
         for m in range(1, place.blocks):
             arrived(self.chunk(place.blk ^ m, 0), self.b_r.at[0, m - 1])
         arrived(self.shard, self.loc.at[0])
-        held = self.full.at[:, place.z, place.core]
+        held = self.lane(place.z, place.core)
         for k in range(1, place.depth):
             target = place.at(place.blk, lax.rem(place.z + k, place.depth), place.core)
             send(held, held, self.z_s.at[k], self.z_r.at[k], target)
         self.pass_on(0)
 
     def pass_on(self, k):
-        held = self.full.at[:, self.level(k), self.place.core]
+        held = self.lane(self.level(k), self.place.core)
         if k > 0:
             arrived(held, self.z_r.at[k])
         send(held, held, self.c_s.at[k], self.c_r.at[k], self.place.sibling())
@@ -467,24 +472,34 @@
         place = self.place
         for k in range(place.depth):
             self.wait_swap(k)
-            arrived(self.full.at[:, 0, 0], self.c_s.at[k])
+            arrived(self.lane(0, 0), self.c_s.at[k])
             if k > 0:
-                arrived(self.full.at[:, 0, 0], self.z_s.at[k])
+                arrived(self.lane(0, 0), self.z_s.at[k])
         for m in range(1, place.blocks):
             arrived(self.shard, self.b_s.at[0, m - 1])
 
 
 def first_kernel(sizes, block, pairs, *refs):
     place = Place(*sizes)
-    tok, vec, w_qkv, w_out, w_up, w_down = refs[:6]
-    att_ref, lse_ref, tok_own, normed_out, qkv_out, cols_out, vec_out, stage, out_full, up_full, down_full = refs[6:17]
-    tok_v, norm_v, norm_t, chunk_v, w32_v, cols_v, qkv_v, kh, vt, run_m, run_l, run_a = refs[17:29]
-    tok_s, tok_r, near_s, near_r, loc = refs[29:34]
-    total = Total(place, *refs[34:38], refs[38:44])
-    qkv = Gather(place, w_qkv, stage, refs[44:51], chunk_v)
-    outw = Gather(place, w_out, out_full, refs[51:58])
-    upw = Gather(place, w_up, up_full, refs[58:65])
-    downw = GatherAcross(place, w_down, down_full, refs[65:72])
+    tok, cot, vec, w_qkv, w_out, w_up, w_down = refs[:7]
+    refs = refs[7:]
+    att_ref, lse_ref, tok_own, cot_own, normed_out, qkv_out, cols_out, vec_out, stage, out_full, up_full, down_full = refs[:12]
+    refs = refs[12:]
+    tok_v, norm_v, norm_t, chunk_v, w32_v, cols_v, qkv_v, kh, vt, run_m, run_l, run_a = refs[:12]
+    tok_s, tok_r, near_s, near_r, cot_s, cot_r, loc = refs[12:19]
+    total = Total(place, *refs[19:23], refs[23:29])
+    refs = refs[29:]
+    late_rows = w_down.shape[0] // 3
+    late_rows = late_rows if late_rows % 16 == 0 else 0
+    early_rows = w_down.shape[0] - late_rows
+    qkv = Gather(place, w_qkv, stage, refs[0:7], chunk_v)
+    outw = Gather(place, w_out, out_full, refs[7:14])
+    upw = Gather(place, w_up, up_full, refs[14:21])
+    downw = GatherAcross(place, w_down, down_full, refs[21:28], span=(0, early_rows))
+    climbers = [outw, upw]
+    if late_rows:
+        climbers.append(Gather(place, w_down, down_full, refs[28:35], span=(early_rows, late_rows)))
+    arrays = [qkv, downw] + climbers
     blocks, depth, seqs, share, bits = place.blocks, place.depth, place.seqs, place.share, place.bits
     blk, z, core, home = place.blk, place.z, place.core, place.home
     pair = pl.program_id(0)
@@ -515,12 +530,12 @@
                     local(tok.at[i], tok_v.at[blk], loc.at[0])
 
         qkv.forward(0, 0)
-        for array in (qkv, outw, upw, downw):
+        for array in arrays:
             array.keep()
         for k in range(1, depth):
             qkv.climb(k)
-        outw.start()
-        upw.start()
+        for array in climbers:
+            array.start()
         total.step(0)
         total.step(1)
 
@@ -545,7 +560,7 @@
                 qkv.step(k, t)
             if t == 0:
                 downw.start()
-        for array in (outw, upw):
+        for array in climbers:
             for k in range(depth):
                 array.climb(k)
         vec_out[...] = total.finish()
@@ -596,13 +611,28 @@
 
     per_pair = count * (count + 1) // 2
     tasks = []
-    levels = [(array, k) for array in (outw, upw) for k in range(depth)]
+    levels = [(array, k) for array in climbers for k in range(depth)]
     for n, (array, k) in enumerate(levels):
         for t in range(bits):
-            where = 0.3 * t + (0.05 + 0.15 * t) * n / len(levels)
+            where = 0.1 + 0.24 * t + (0.15 + 0.35 * t) * n / len(levels)
             tasks.append((where, functools.partial(array.step, k, t)))
     for k in range(1, depth):
-        tasks.append((0.6 + 0.25 * k / depth, functools.partial(downw.pass_on, k)))
+        tasks.append((0.55 + 0.3 * k / depth, functools.partial(downw.pass_on, k)))
+
+    def own_rows():
+        for i in range(seqs):
+            owner = (core * seqs + i) * share + blk // place.per_part
+            slot = lax.rem(blk, place.per_part)
+
+            @pl.when(owner != blk * 2 + core)
+            def _(i=i, owner=owner, slot=slot):
+                send(cot.at[i], cot_own.at[slot], cot_s.at[i], cot_r.at[slot], place.at(owner // 2, z, owner % 2))
+
+            @pl.when(owner == blk * 2 + core)
+            def _(i=i, slot=slot):
+                local(cot.at[i], cot_own.at[slot], loc.at[4 + place.per_part])
+
+    tasks.append((0.28, own_rows))
     tasks.sort(key=lambda task: task[0])
     todo = plan(tasks, pairs * per_pair)
 
@@ -621,9 +651,11 @@
         def one(kj, masked):
             at = pl.ds(pl.multiple_of(kj * block, block), block)
             q_rows = qkv_v[at_q, lanes_of(0)]
+            scores = [dot_nt(kh[h, at, :], q_rows) for h in range(2)]
+            weighed = []
             for h in range(2):
                 peak, so_far = run_m[h : h + 1, :], run_l[h : h + 1, :]
-                s = dot_nt(kh[h, at, :], q_rows)
+                s = scores[h]
                 u = s * s + 1.0
                 inv = lax.rsqrt(u)
                 mag = u * inv
@@ -634,7 +666,9 @@
                 alpha = jnp.exp(peak - new)
                 run_m[h : h + 1, :] = new
                 run_l[h : h + 1, :] = so_far * alpha + jnp.sum(p, axis=0, keepdims=True)
-                signed = (p * (s * inv)).astype(jnp.bfloat16)
+                weighed.append((alpha, (p * (s * inv)).astype(jnp.bfloat16)))
+            for h in range(2):
+                alpha, signed = weighed[h]
                 head = slice(64 * h, 64 * h + 64)
                 run_a[head, :] = run_a[head, :] * alpha + dot_nn(vt[head, at], signed)
 
@@ -662,8 +696,25 @@
 
     @pl.when(pair == pairs - 1)
     def _():
-        for array in (qkv, outw, upw, downw):
+        for array in arrays:
             array.finish()
+        for i in range(seqs):
+
+            @pl.when((core * seqs + i) * share + blk // place.per_part != blk * 2 + core)
+            def _(i=i):
+                arrived(cot.at[i], cot_s.at[i])
+
+        for t in range(place.per_part):
+            here = (place.part * place.per_part + t == blk) & (home == core)
+
+            @pl.when(here)
+            def _(t=t):
+                arrived(cot_own.at[t], loc.at[4 + place.per_part])
+
+            @pl.when(jnp.logical_not(here))
+            def _(t=t):
+                arrived(cot_own.at[t], cot_r.at[t])
+
         arrived(norm_t, loc.at[1])
         arrived(cols_v, loc.at[2 + place.per_part])
         arrived(qkv_v, loc.at[3 + place.per_part])
@@ -688,7 +739,7 @@
                     arrived(tok_v.at[blk], loc.at[0])
 
 
-def first_half(sizes, tok, vec, w_qkv, w_out, w_up, w_down, block):
+def first_half(sizes, tok, cot, vec, w_qkv, w_out, w_up, w_down, block):
     blocks, lanes, seqs = sizes
     depth, share = lanes // 2, blocks // seqs
     per_part = blocks // share
@@ -707,6 +758,7 @@
             shape((length, 128 * pairs), low),
             shape((pairs, 8, length), full),
             shape((per_part, rows, model), low),
+            shape((per_part, rows, model), low),
             shape((model, length), low),
             shape((length, width), low),
             shape((model, width), low),
@@ -716,9 +768,9 @@
             shape(owners + w_up.shape, low),
             shape(owners + w_down.shape, low),
         ],
-        in_specs=[ANYWHERE, in_vmem] + [ANYWHERE] * 4,
+        in_specs=[ANYWHERE, ANYWHERE, in_vmem] + [ANYWHERE] * 4,
         out_specs=[pl.BlockSpec((length, 128), lambda p: (0, p)), pl.BlockSpec((1, 8, length), lambda p: (p, 0, 0))]
-        + [ANYWHERE] * 4
+        + [ANYWHERE] * 5
         + [in_vmem]
         + [ANYWHERE] * 4,
         scratch_shapes=[
@@ -738,12 +790,14 @@
             DMA((blocks,)),
             DMA((blocks,)),
             DMA((blocks,)),
-            DMA((4 + per_part,)),
+            DMA((seqs,)),
+            DMA((per_part,)),
+            DMA((5 + per_part,)),
         ]
         + Total.scratch(sizes, vec.shape)
-        + Gather.sems(sizes) * 4,
+        + Gather.sems(sizes) * 5,
         compiler_params=pltpu.CompilerParams(collective_id=0, has_side_effects=True, vmem_limit_bytes=VMEM_LIMIT),
-    )(tok, vec, w_qkv, w_out, w_up, w_down)
+    )(tok, cot, vec, w_qkv, w_out, w_up, w_down)
 
 
 def dot_tn(left, right):
@@ -780,7 +834,7 @@
     result, g_heads, g_mid, g_out, g_up, g_down, g_vec = refs[8:15]
     (att_v, tok_v, cot_v, res_v, out_v, up_v, down_v, mid_v, n2_v, n2t_v, hid_v, slope_v, sum_v, ga_v) = refs[15:29]
     (st_out, st_up, st_down) = refs[29:32]
-    a_s, a_r, g_s, g_r, cot_s, cot_r, m_s, m_r, loc, up_l, down_l, o_l = refs[32:]
+    a_s, a_r, g_s, g_r, m_s, m_r, loc, up_l, down_l, o_l = refs[32:]
     share, per_part, seqs = place.share, place.per_part, place.seqs
     part, blk, z, core = place.part, place.blk, place.z, place.core
     rows, model = mid_v.shape
@@ -801,17 +855,7 @@
     for t in range(per_part):
         local(tok_own.at[t], tok_v.at[t], loc.at[1 + t])
     local(w_out, out_v, loc.at[1 + per_part])
-    for i in range(seqs):
-        owner = (core * seqs + i) * share + blk // per_part
-        slot = lax.rem(blk, per_part)
-
-        @pl.when(owner != flat)
-        def _(i=i, owner=owner, slot=slot):
-            send(cot.at[i], cot_v.at[slot], cot_s.at[i], cot_r.at[slot], place.at(owner // 2, z, owner % 2))
-
-        @pl.when(owner == flat)
-        def _(i=i, slot=slot):
-            local(cot.at[i], cot_v.at[slot], loc.at[2 + per_part])
+    local(cot, cot_v, loc.at[2 + per_part])
 
     def span(f):
         return pl.ds(pl.multiple_of(f * chunk, chunk), chunk)
@@ -873,17 +917,7 @@
         def _(t=t, source=source):
             send(res_v.at[t], result.at[slot_of], m_s.at[t], m_r.at[slot_of], place.at(source, z, place.home))
 
-    for t in range(per_part):
-        mine = (part * per_part + t == blk) & (place.home == core)
-
-        @pl.when(mine)
-        def _(t=t):
-            arrived(cot_v.at[t], loc.at[2 + per_part])
-
-        @pl.when(jnp.logical_not(mine))
-        def _(t=t):
-            arrived(cot_v.at[t], cot_r.at[t])
-
+    arrived(cot_v, loc.at[2 + per_part])
     sum_v[...] = jnp.zeros_like(sum_v)
 
     def back_step(f, _):
@@ -948,7 +982,6 @@
 
         @pl.when(owner != flat)
         def _(i=i):
-            arrived(cot.at[i], cot_s.at[i])
             arrived(result.at[i], m_r.at[i])
 
     for t in range(per_part):
@@ -1009,8 +1042,6 @@
             DMA((share,)),
             DMA((share,)),
             DMA((share,)),
-            DMA((seqs,)),
-            DMA((per_part,)),
             DMA((per_part,)),
             DMA((seqs,)),
             DMA((3 + per_part,)),
@@ -1051,20 +1082,22 @@
 
     tasks = []
     units = [(a, k) for a in range(3) for k in fold.order]
-    scale = 12.0 / len(units) / 80.0
+    per = 12.0 / len(units)
     for n, (a, k) in enumerate(units):
-        tasks.append(((3 + 1.3 * n) * scale, functools.partial(fold.join, a, k)))
+        tasks.append((8 + 1.2 * per * n, functools.partial(fold.join, a, k)))
         for t in range(bits):
-            where = 8 + 6 * t + (3.2 + 0.4 * t) * n
-            tasks.append((where * scale, functools.partial(fold.step, a, k, t)))
+            where = (14 + 2.7 * per * n) if t == 0 else (38 + 8 * t + 1.4 * per * n)
+            tasks.append((where, functools.partial(fold.step, a, k, t)))
     for a in range(3):
-        tasks.append((0.78 + 0.05 * a, functools.partial(fold.total, a)))
+        tasks.append((72 + 2 * a, functools.partial(fold.total, a)))
     for p in range(pairs - 1):
+        third = 85.0 / pairs
         for n, k in enumerate(fold.order):
-            tasks.append(((p + 1.15) / pairs, functools.partial(fold.join, 3 + p, k)))
+            tasks.append(((p + 1.1) * third, functools.partial(fold.join, 3 + p, k)))
             for t in range(bits):
-                where = p + 1.4 + 0.5 * t / bits + 0.1 * n / depth
-                tasks.append((where / pairs, functools.partial(fold.step, 3 + p, k, t)))
+                where = (68 if p == pairs - 2 else 60) + 6 * t
+                tasks.append((where, functools.partial(fold.step, 3 + p, k, t)))
+    tasks = [(where / 85.0, call) for where, call in tasks]
     tasks.sort(key=lambda task: task[0])
     todo = plan(tasks, pairs * per_pair)
 
@@ -1097,9 +1130,9 @@
             q_rows = q_ref[at_q, :]
             g_rows = g_ref[at_q, :]
             add_k = add_v = None
+            both = [(dot_nt(kh[h, at, :], q_rows), dot_nt(vh[h, at, :], g_rows)) for h in range(2)]
             for h in range(2):
-                s = dot_nt(kh[h, at, :], q_rows)
-                dp = dot_nt(vh[h, at, :], g_rows)
+                s, dp = both[h]
                 u = s * s + 1.0
                 inv = lax.rsqrt(u)
                 arg = u * inv - lse_ref[0, h : h + 1, at_q]
@@ -1146,18 +1179,23 @@
         arrived(mid_v, loc.at[2])
         arrived(tok_v, loc.at[3])
 
-    sum_v[...] = dot_nn(norm_v[...], gq_v[pair])
-    for b in range(blocks):
-        for d in range(depth):
-            for c in range(2):
-                first = ((b * depth + d) * 2 + c) * owned
-                own_v[pair, b, d, c] = sum_v[first : first + owned, :].astype(jnp.bfloat16)
-    for p in range(pairs):
-
-        @pl.when(pair == p)
-        def _(p=p):
-            for k in fold.order:
-                fold.start(3 + p, k)
+    def weight_grad():
+        sum_v[...] = dot_nn(norm_v[...], gq_v[pair])
+        for b in range(blocks):
+            for d in range(depth):
+                for c in range(2):
+                    first = ((b * depth + d) * 2 + c) * owned
+                    own_v[pair, b, d, c] = sum_v[first : first + owned, :].astype(jnp.bfloat16)
+        for p in range(pairs):
+
+            @pl.when(pair == p)
+            def _(p=p):
+                for k in fold.order:
+                    fold.start(3 + p, k)
+
+    @pl.when(pair != pairs - 1)
+    def _():
+        weight_grad()
 
     @pl.when(pair == pairs - 1)
     def _():
@@ -1171,21 +1209,24 @@
                 value = value + dot_nt(gq_v[p, at, :], cols_v[:, p * 384 : (p + 1) * 384])
             return value
 
-        for k in range(1, share):
-
-            def away(i, _, k=k):
-                at = pl.ds(pl.multiple_of(i * tile, tile), tile)
-                part_v[k - 1, at, :] = input_grad(part ^ k, i).astype(jnp.bfloat16)
-                return 0
-
-            lax.fori_loop(0, rows // tile, away, 0)
-            send(part_v.at[k - 1], got_v.at[k - 1], p_s.at[k - 1], p_r.at[k - 1], place.at(*partners[k - 1]))
-        for k in fold.order:
-            fold.join(mine, k)
+        per_block = rows // per_part // tile
+        half = rows // per_part
+        for t in range(per_part):
+            for k in range(1, share):
+
+                def away(i, _, k=k):
+                    at = pl.ds(pl.multiple_of(i * tile, tile), tile)
+                    part_v[k - 1, at, :] = input_grad(part ^ k, i).astype(jnp.bfloat16)
+                    return 0
+
+                lax.fori_loop(t * per_block, (t + 1) * per_block, away, 0)
+                piece = pl.ds(t * half, half)
+                sems = p_s.at[k - 1, t], p_r.at[k - 1, t]
+                send(part_v.at[k - 1, piece], got_v.at[k - 1, piece], *sems, place.at(*partners[k - 1]))
+        weight_grad()
         total.stages[0] = jnp.zeros(total.stages.shape[1:], jnp.float32)
         total.stages[0, 2:4, :] = two[0:2, :]
         gain = vec[0:1, :]
-        per_block = rows // per_part // tile
 
         def leave(i, _):
             at = pl.ds(pl.multiple_of(i * tile, tile), tile)
@@ -1200,9 +1241,9 @@
             out_v[t, inside, :] = (mid_v[at, :] + back).astype(jnp.bfloat16)
             return 0
 
-        for k in range(1, share):
-            arrived(got_v.at[k - 1], p_r.at[k - 1])
         for t in range(per_part):
+            for k in range(1, share):
+                arrived(got_v.at[k - 1, pl.ds(t * half, half)], p_r.at[k - 1, t])
             lax.fori_loop(t * per_block, (t + 1) * per_block, leave, 0)
             source = part * per_part + t
             here = (source == blk) & (place.home == core)
@@ -1217,19 +1258,20 @@
 
             if t == 0:
                 for k in fold.order:
-                    fold.step(mine, k, 0)
+                    fold.join(mine, k)
         total.start()
-        for t in range(1, bits):
+        for t in range(bits):
             for k in fold.order:
                 fold.step(mine, k, t)
-        for n in range(bits + 1):
-            total.step(n)
+            total.step(t)
+        total.step(bits)
         for p in range(pairs):
             fold.total(3 + p)
         vec_out[...] = total.finish()
         fold.finish()
         for k in range(1, share):
-            arrived(part_v.at[k - 1], p_s.at[k - 1])
+            for t in range(per_part):
+                arrived(part_v.at[k - 1, pl.ds(t * half, half)], p_s.at[k - 1, t])
         for t in range(per_part):
             here = (part * per_part + t == blk) & (place.home == core)
 
@@ -1290,8 +1332,8 @@
             pltpu.VMEM((share - 1, rows, model), low),
             pltpu.VMEM((share - 1, rows, model), low),
             pltpu.VMEM((model, 384), full),
-            DMA((share,)),
-            DMA((share,)),
+            DMA((share, per_part)),
+            DMA((share, per_part)),
             DMA((per_part,)),
             DMA((seqs,)),
             DMA((4,)),
@@ -1323,8 +1365,8 @@
     vec = lax.dynamic_update_slice(vec, own, (0, flat * owned))
     first = (place.blk == 0).astype(jnp.float32)
     vec = lax.dynamic_update_slice(vec, first * seq_len.astype(jnp.float32)[None], (4, lax.axis_index("seq") * seqs))
-    outs = first_half(sizes, tokens, vec, grouped, w_out, w_up, w_down, min(512, rows))
-    att, lse, tok_own, norm_t, qkv, qkv_cols, params, _, out_full, up_full, down_full = outs
+    outs = first_half(sizes, tokens, cotangent, vec, grouped, w_out, w_up, w_down, min(512, rows))
+    att, lse, tok_own, cot_own, norm_t, qkv, qkv_cols, params, _, out_full, up_full, down_full = outs
     out_full, up_full = [a.reshape(model, -1) for a in (out_full, up_full)]
     down_full = down_full.reshape(-1, model)
     my_len = lax.dynamic_index_in_dim(params[4], place.z * 2 * seqs + place.seq, 0, False)
@@ -1336,14 +1378,14 @@
         cols,
         att.reshape(share, rows, wide),
         tok_own,
-        cotangent,
+        cot_own,
         out_full,
         up_full,
         down_full,
         params,
         live,
-        min(256, tokens.shape[1]),
-        min(512, w_up.shape[1]),
+        min(512, tokens.shape[1]),
+        min(1024, w_up.shape[1]),
     )
 
     def cut(values):

time: 340 us -> 340 us (level)
  no operation moved by 1% of the time
where the time goes in v1:
time: 340 us; the launch traced here: 337 us
  Pallas kernels  319 us (94%)
  local copies, waits for them, and re-layouts  12.1 us (4%)
  other arithmetic  4.87 us (1%)
    pallas_call x1, Pallas kernels, last_half(): pl.pallas_call(functools.partial(last_kernel, sizes, block, pairs), grid=...  145 us
    pallas_call x1, Pallas kernels, first_half(): pl.pallas_call(functools.partial(first_kernel, sizes, block, pairs), grid...  121 us
    pallas_call x1, Pallas kernels, feed_forward(): pl.pallas_call(functools.partial(mlp_kernel, sizes, cols, tile, chunk), o...  53.5 us

profile of v1, /device:TPU:0, one launch (start us, length us, event | category | flops | bytes accessed | tf_op | source)
XLA Modules:
  0.0 337.3 jit_solution(14607804688645229570)
XLA Ops:
  0.7 0.7 multiply_bitcast_fusion
  1.4 0.7 maximum_convert_fusion
  2.1 0.4 dynamic_update_slice.6
  2.5 0.2 dynamic_update_slice.7.refs_2_
  2.7 1.0 reshape.78
  3.8 0.7 reshape.79.refs_3_
  4.5 120.7 %shard_map.186 = (bf16[2048,384]{1,0:T(8,128)(2,1)}, f32[3,8,2048]{2,1,0:T(8,128)}, bf16[2,512,768]{2,1,0:T(8,128)(2,1)}, bf16[2,512,768]{2,1,0:T(8,128)(2,1)}, ...) custom-call(bf16[2,512,768]{2,1,0:T(8,128)(2,1)} %refs_0_.1, ...), custom_call_target="tpu_custom_call" | custom-call | tf_op jit(solution)/shard_map/pallas_call | solution.py:754
  125.2 0.7 slice.15
  125.9 0.6 constant_dynamic-slice_fusion.1
  126.5 1.5 fusion.refs_7_
  128.0 53.5 %shard_map.187 = (bf16[2,512,768]{2,1,0:T(8,128)(2,1)}, bf16[2,1024,384]{2,1,0:T(8,128)(2,1)}, f32[1024,768]{1,0:T(8,128)}, bf16[768,768]{1,0:T(8,128)(2,1)}, bf...) custom-call(bf16[2,1024,384]{2,1,0:T(8,128)(2,1)} %bitcast.26, ...), custom_call_target="tpu_custom_call" | custom-call | tf_op jit(solution)/shard_map/pallas_call | solution.py:1010
  181.5 145.1 %shard_map.188 = (f32[24,768]{1,0:T(8,128)}, f32[24,3072]{1,0:T(8,128)}, f32[96,768]{1,0:T(8,128)}, f32[2,24,384]{2,1,0:T(8,128)}, f32[2,24,384]{2,1,0:T(8,128)}...) custom-call(bf16[2048,1152]{1,0:T(8,128)(2,1)} %get-tuple-element.44.refs_0_.refs_1_.refs_2_, ...), custom_call_target="tpu_custom_call" | custom-call | tf_op jit(solution)/shard_map/pallas_call | solution.py:1308
  326.7 0.9 constant_dynamic-slice_fusion
  327.6 0.5 slice_bitcast_fusion
  328.1 0.9 stack.32
  329.0 0.9 stack.33
  329.9 0.9 stack.34
  330.9 0.2 copy.27
  331.1 0.8 reshape_reshape.3
  331.9 1.9 convert_element_type.37
  333.9 1.1 copy.34
  335.0 0.6 copy.35
  335.6 0.7 copy.36
  336.4 0.7 copy.37
  (15 shorter events, 0.2 us)
Async XLA Ops:
  2.7 1.8 copy-start.4
  326.7 5.2 %copy-start.1 = (bf16[2,512,768]{2,1,0:T(8,128)(2,1)S(1)}, bf16[2,512,768]{2,1,0:T(8,128)(2,1)}, u32[]{:S(2)}) copy-start(bf16[2,512,768]{2,1,0:T(8,128)(2,1)} %get-tuple-element.54) | copy-start | bytes 4718596
  331.9 2.0 copy-start
  333.9 1.2 copy-start.5
  333.9 1.8 copy-start.3
  333.9 2.5 copy-start.2

commit v2 on v1

--- a/solution.py
+++ b/solution.py
@@ -189,12 +189,15 @@
             send(block, self.tall[a].at[k - 1], *sems, place.at(place.blk, self.level(k), place.core))
 
     def total(self, a):
+        self.sums[a][...] = self.value(a)
+
+    def value(self, a):
         place = self.place
         value = self.held[a][place.blk, place.z].astype(jnp.float32)
         for k in range(1, place.depth):
             arrived(self.tall[a].at[k - 1], self.z_r.at[a, k - 1])
             value = value + self.tall[a][k - 1].astype(jnp.float32)
-        self.sums[a][...] = value
+        return value
 
     def rows(self, j):
         place = self.place
@@ -483,12 +486,12 @@
     place = Place(*sizes)
     tok, cot, vec, w_qkv, w_out, w_up, w_down = refs[:7]
     refs = refs[7:]
-    att_ref, lse_ref, tok_own, cot_own, normed_out, qkv_out, cols_out, vec_out, stage, out_full, up_full, down_full = refs[:12]
-    refs = refs[12:]
-    tok_v, norm_v, norm_t, chunk_v, w32_v, cols_v, qkv_v, kh, vt, run_m, run_l, run_a = refs[:12]
-    tok_s, tok_r, near_s, near_r, cot_s, cot_r, loc = refs[12:19]
-    total = Total(place, *refs[19:23], refs[23:29])
-    refs = refs[29:]
+    att_ref, lse_ref, att_own, tok_own, cot_own, normed_out, qkv_out, cols_out, vec_out, stage, out_full, up_full, down_full = refs[:13]
+    refs = refs[13:]
+    tok_v, norm_v, norm_t, chunk_v, w32_v, cols_v, qkv_v, kh, vt, run_m, run_l, run_a, att_v = refs[:13]
+    tok_s, tok_r, near_s, near_r, cot_s, cot_r, a_s, a_r, loc = refs[13:22]
+    total = Total(place, *refs[22:26], refs[26:32])
+    refs = refs[32:]
     late_rows = w_down.shape[0] // 3
     late_rows = late_rows if late_rows % 16 == 0 else 0
     early_rows = w_down.shape[0] - late_rows
@@ -560,9 +563,6 @@
                 qkv.step(k, t)
             if t == 0:
                 downw.start()
-        for array in climbers:
-            for k in range(depth):
-                array.climb(k)
         vec_out[...] = total.finish()
         gain, shift = vec_out[0:1, :], vec_out[1:2, :]
         part_rows = min(rows, 128)
@@ -587,6 +587,9 @@
         for t in range(place.per_part):
             local(tok_v.at[place.part * place.per_part + t], tok_own.at[t], loc.at[2 + t])
         downw.climb()
+        for array in climbers:
+            for k in range(depth):
+                array.climb(k)
         for k in range(depth):
             qkv.wait_swap(k)
         for b in range(blocks):
@@ -614,7 +617,7 @@
     levels = [(array, k) for array in climbers for k in range(depth)]
     for n, (array, k) in enumerate(levels):
         for t in range(bits):
-            where = 0.1 + 0.24 * t + (0.15 + 0.35 * t) * n / len(levels)
+            where = 0.08 + 0.26 * t + (0.1 + 0.25 * t) * n / len(levels)
             tasks.append((where, functools.partial(array.step, k, t)))
     for k in range(1, depth):
         tasks.append((0.55 + 0.3 * k / depth, functools.partial(downw.pass_on, k)))
@@ -632,7 +635,7 @@
             def _(i=i, slot=slot):
                 local(cot.at[i], cot_own.at[slot], loc.at[4 + place.per_part])
 
-    tasks.append((0.28, own_rows))
+    tasks.append((0.2, own_rows))
     tasks.sort(key=lambda task: task[0])
     todo = plan(tasks, pairs * per_pair)
 
@@ -689,13 +692,35 @@
         for h in range(2):
             both.append(run_a[64 * h : 64 * h + 64, :] / run_l[h : h + 1, :])
             lse_ref[0, h : h + 1, at_q] = run_m[h : h + 1, :] + jnp.log(run_l[h : h + 1, :])
-        att_ref[at_q, :] = jnp.concatenate(both, 0).T.astype(jnp.bfloat16)
+        joined = jnp.concatenate(both, 0).T.astype(jnp.bfloat16)
+        att_ref[at_q, :] = joined
+        att_v[pair, at_q, :] = joined
         return 0
 
     lax.fori_loop(0, count, q_step, 0)
+    part, mine = place.part, length // share
+    flat = blk * 2 + core
+
+    def piece(p, g):
+        return att_v.at[p, pl.ds(pl.multiple_of(g * mine, 16), mine)]
+
+    for p in range(pairs):
+        there = att_own.at[part, :, pl.ds(p * 128, 128)]
+
+        @pl.when(pair == p)
+        def _(p=p, there=there):
+            for k in range(1, share):
+                other = flat ^ k
+                send(piece(p, part ^ k), there, a_s.at[k, p], a_r.at[k, p], place.at(other // 2, z, other % 2))
+            local(piece(p, part), there, a_s.at[0, p])
 
     @pl.when(pair == pairs - 1)
     def _():
+        for p in range(pairs):
+            for k in range(share):
+                arrived(piece(p, 0), a_s.at[k, p])
+                if k > 0:
+                    arrived(att_own.at[part ^ k, :, pl.ds(p * 128, 128)], a_r.at[k, p])
         for array in arrays:
             array.finish()
         for i in range(seqs):
@@ -757,6 +782,7 @@
         out_shape=[
             shape((length, 128 * pairs), low),
             shape((pairs, 8, length), full),
+            shape((share, length // share, 128 * pairs), low),
             shape((per_part, rows, model), low),
             shape((per_part, rows, model), low),
             shape((model, length), low),
@@ -770,7 +796,7 @@
         ],
         in_specs=[ANYWHERE, ANYWHERE, in_vmem] + [ANYWHERE] * 4,
         out_specs=[pl.BlockSpec((length, 128), lambda p: (0, p)), pl.BlockSpec((1, 8, length), lambda p: (p, 0, 0))]
-        + [ANYWHERE] * 5
+        + [ANYWHERE] * 6
         + [in_vmem]
         + [ANYWHERE] * 4,
         scratch_shapes=[
@@ -786,12 +812,15 @@
             pltpu.VMEM((8, block), full),
             pltpu.VMEM((8, block), full),
             pltpu.VMEM((128, block), full),
+            pltpu.VMEM((pairs, length, 128), low),
             DMA((seqs * share // 2,)),
             DMA((blocks,)),
             DMA((blocks,)),
             DMA((blocks,)),
             DMA((seqs,)),
             DMA((per_part,)),
+            DMA((share, pairs)),
+            DMA((share, pairs)),
             DMA((5 + per_part,)),
         ]
         + Total.scratch(sizes, vec.shape)
@@ -830,11 +859,12 @@
 
 def mlp_kernel(sizes, cols, tile, chunk, *refs):
     place = Place(*sizes)
-    att, tok_own, cot, w_out, w_up, w_down, vec, live = refs[:8]
-    result, g_heads, g_mid, g_out, g_up, g_down, g_vec = refs[8:15]
-    (att_v, tok_v, cot_v, res_v, out_v, up_v, down_v, mid_v, n2_v, n2t_v, hid_v, slope_v, sum_v, ga_v) = refs[15:29]
-    (st_out, st_up, st_down) = refs[29:32]
-    a_s, a_r, g_s, g_r, m_s, m_r, loc, up_l, down_l, o_l = refs[32:]
+    att, tok_own, cot, w_out, w_up, w_down, vec = refs[:7]
+    refs = refs[7:]
+    result, g_heads, g_mid, g_out, g_up, g_down, g_vec = refs[:7]
+    (att_v, tok_v, cot_v, res_v, out_v, up_v, down_v, mid_v, n2_v, n2t_v, hid_v, slope_v, sum_v, ga_v) = refs[7:21]
+    (st_out, st_up, st_down) = refs[21:24]
+    g_s, g_r, m_s, m_r, loc, up_l, down_l, o_l = refs[24:]
     share, per_part, seqs = place.share, place.per_part, place.seqs
     part, blk, z, core = place.part, place.blk, place.z, place.core
     rows, model = mid_v.shape
@@ -845,13 +875,10 @@
     partners = [((flat ^ k) // 2, z, (flat ^ k) % 2) for k in range(1, share)]
     slot_of = lax.rem(place.seq, seqs)
     greet(place.peers(False, True))
-    for k in range(1, share):
-        send(att.at[part ^ k], att_v.at[part], a_s.at[k - 1], a_r.at[k - 1], place.at(*partners[k - 1]))
-
     def local(src, dst, sem):
         pltpu.make_async_copy(src, dst, sem).start()
 
-    local(att.at[part], att_v.at[part], loc.at[0])
+    local(att, att_v, loc.at[0])
     for t in range(per_part):
         local(tok_own.at[t], tok_v.at[t], loc.at[1 + t])
     local(w_out, out_v, loc.at[1 + per_part])
@@ -864,17 +891,23 @@
         local(w_up.at[:, pl.ds(f * chunk, chunk)], up_v.at[:, pl.ds(f * chunk, chunk)], up_l.at[f])
         local(w_down.at[pl.ds(f * chunk, chunk)], down_v.at[pl.ds(f * chunk, chunk)], down_l.at[f])
 
-    arrived(att_v.at[part], loc.at[0])
+    arrived(att_v, loc.at[0])
     for t in range(per_part):
         arrived(tok_v.at[t], loc.at[1 + t])
     arrived(out_v, loc.at[1 + per_part])
-    for k in range(1, share):
-        arrived(att_v.at[part ^ k], a_r.at[k - 1])
     gain, shift = vec[2:3, :], vec[3:4, :]
     per_block = block // tile
 
     def spot(i):
         return i // per_block, pl.ds(pl.multiple_of(lax.rem(i, per_block) * tile, tile), tile)
+
+    lane = lax.broadcasted_iota(jnp.int32, (1, model), 1)
+    mine_at = z * 2 * seqs + place.seq
+    length = jnp.sum(jnp.where(lane == mine_at, vec[4:5, :], 0.0), axis=1, keepdims=True)
+
+    def live(i):
+        position = part * rows + i * tile + lax.broadcasted_iota(jnp.int32, (tile, 1), 0)
+        return jnp.where(position.astype(jnp.float32) < length, 1.0, 0.0)
 
     def enter(i, _):
         at = pl.ds(pl.multiple_of(i * tile, tile), tile)
@@ -882,7 +915,7 @@
         for g in range(1, share):
             branch = branch + dot_nn(att_v[g, at, :cols], out_v[g * cols : (g + 1) * cols, :])
         t, inside = spot(i)
-        middle = tok_v[t, inside, :].astype(jnp.float32) + live[at, :] * branch
+        middle = tok_v[t, inside, :].astype(jnp.float32) + live(i) * branch
         mid_v[at, :] = middle
         unit, _ = centered(middle)
         normed = unit * gain + shift
@@ -948,7 +981,7 @@
         g_vec[1:2, :] += d_shift
         total = cot_v[t, inside, :].astype(jnp.float32) + back
         mid_v[at, :] = total
-        branch = (live[at, :] * total).astype(jnp.bfloat16)
+        branch = (live(i) * total).astype(jnp.bfloat16)
         n2_v[at, :] = branch
         heads = dot_nt(branch, out_v[...]).astype(jnp.bfloat16)
         for g in range(share):
@@ -974,7 +1007,6 @@
     arrived(mid_v, loc.at[2])
     arrived(ga_v.at[part], loc.at[1])
     for k in range(1, share):
-        arrived(att.at[part ^ k], a_s.at[k - 1])
         arrived(ga_v.at[part ^ k], g_s.at[k - 1])
         arrived(g_heads.at[part ^ k], g_r.at[k - 1])
     for i in range(seqs):
@@ -996,7 +1028,7 @@
             arrived(res_v.at[t], m_s.at[t])
 
 
-def feed_forward(sizes, cols, att, tok_own, cot, w_out, w_up, w_down, vec, live, tile, chunk):
+def feed_forward(sizes, cols, att, tok_own, cot, w_out, w_up, w_down, vec, tile, chunk):
     blocks, lanes, seqs = sizes
     share = blocks // seqs
     per_part = blocks // share
@@ -1018,7 +1050,7 @@
             jax.ShapeDtypeStruct((ff, model), low),
             jax.ShapeDtypeStruct((8, model), full),
         ],
-        in_specs=[ANYWHERE] * 6 + [in_vmem] * 2,
+        in_specs=[ANYWHERE] * 6 + [in_vmem],
         out_specs=[ANYWHERE] * 6 + [in_vmem],
         scratch_shapes=[
             pltpu.VMEM((share, rows, wide), low),
@@ -1040,8 +1072,6 @@
             pltpu.VMEM((2, chunk, model), low),
             DMA((share,)),
             DMA((share,)),
-            DMA((share,)),
-            DMA((share,)),
             DMA((per_part,)),
             DMA((seqs,)),
             DMA((3 + per_part,)),
@@ -1050,7 +1080,7 @@
             DMA((4,)),
         ],
         compiler_params=pltpu.CompilerParams(collective_id=4, has_side_effects=True, vmem_limit_bytes=VMEM_LIMIT),
-    )(att, tok_own, cot, w_out, w_up, w_down, vec, live)
+    )(att, tok_own, cot, w_out, w_up, w_down, vec)
 
 
 def last_kernel(sizes, block, pairs, *refs):
@@ -1062,7 +1092,7 @@
     q_ref, k_ref, v_ref, g_ref, att_ref, lse_ref = refs[:6]
     big, tok_own, g_mid, norm_t, cols, vec, two = refs[6:9], refs[9], refs[10], refs[11], refs[12], refs[13], refs[14]
     refs = refs[15:]
-    sums, tok_out, vec_out, refs = refs[:count], refs[count], refs[count + 1], refs[count + 2 :]
+    sums, qkv_sum, tok_out, vec_out, refs = refs[:3], refs[3], refs[4], refs[5], refs[6:]
     kh, vh, qh, gh, kt, delta, dqt, dk, dv = refs[:9]
     gq_v, own_v, norm_v, cols_v, tok_v, mid_v, out_v, part_v, got_v, sum_v = refs[9:19]
     p_s, p_r, t_s, t_r, loc = refs[19:24]
@@ -1266,7 +1296,11 @@
             total.step(t)
         total.step(bits)
         for p in range(pairs):
-            fold.total(3 + p)
+            value = fold.value(3 + p)
+            for g in range(share):
+                for n in range(3):
+                    first = ((n * share + g) * pairs + p) * 128
+                    qkv_sum[:, first : first + 128] = value[g, :, n * 128 : n * 128 + 128]
         vec_out[...] = total.finish()
         fold.finish()
         for k in range(1, share):
@@ -1308,13 +1342,18 @@
     return pl.pallas_call(
         functools.partial(last_kernel, sizes, block, pairs),
         grid=(pairs,),
-        out_shape=out + [jax.ShapeDtypeStruct((seqs, rows_in, model), low), jax.ShapeDtypeStruct(vec.shape, full)],
+        out_shape=out[:3]
+        + [
+            jax.ShapeDtypeStruct((owned, share * width), full),
+            jax.ShapeDtypeStruct((seqs, rows_in, model), low),
+            jax.ShapeDtypeStruct(vec.shape, full),
+        ],
         in_specs=[pl.BlockSpec((length, 128), lambda p, n=n: (0, 3 * p + n)) for n in range(3)]
         + [pl.BlockSpec((length, 128), lambda p: (0, p))] * 2
         + [pl.BlockSpec((1, 8, length), lambda p: (p, 0, 0))]
         + [ANYWHERE] * 7
         + [in_vmem] * 2,
-        out_specs=[in_vmem] * len(out) + [ANYWHERE, in_vmem],
+        out_specs=[in_vmem] * 4 + [ANYWHERE, in_vmem],
         scratch_shapes=[pltpu.VMEM((2, length, 128), low)] * 4
         + [
             pltpu.VMEM((128, length), low),
@@ -1366,24 +1405,19 @@
     first = (place.blk == 0).astype(jnp.float32)
     vec = lax.dynamic_update_slice(vec, first * seq_len.astype(jnp.float32)[None], (4, lax.axis_index("seq") * seqs))
     outs = first_half(sizes, tokens, cotangent, vec, grouped, w_out, w_up, w_down, min(512, rows))
-    att, lse, tok_own, cot_own, norm_t, qkv, qkv_cols, params, _, out_full, up_full, down_full = outs
+    att, lse, att_own, tok_own, cot_own, norm_t, qkv, qkv_cols, params, _, out_full, up_full, down_full = outs
     out_full, up_full = [a.reshape(model, -1) for a in (out_full, up_full)]
     down_full = down_full.reshape(-1, model)
-    my_len = lax.dynamic_index_in_dim(params[4], place.z * 2 * seqs + place.seq, 0, False)
-
-    positions = part * rows + jnp.arange(rows, dtype=jnp.int32)
-    live = (positions.astype(jnp.float32) < my_len).astype(jnp.float32)[:, None]
     result, g_heads, grad_mid, grad_out, grad_up, grad_down, two_grads = feed_forward(
         sizes,
         cols,
-        att.reshape(share, rows, wide),
+        att_own,
         tok_own,
         cot_own,
         out_full,
         up_full,
         down_full,
         params,
-        live,
         min(512, tokens.shape[1]),
         min(1024, w_up.shape[1]),
     )
@@ -1406,10 +1440,10 @@
         two_grads,
         min(512, rows),
     )
-    sum_out, sum_up, sum_down, *sum_pairs, grad_tokens, vec_sum = done
+    sum_out, sum_up, sum_down, sum_qkv, grad_tokens, vec_sum = done
     vec_own = lax.dynamic_slice_in_dim(vec_sum, flat * owned, owned, 1)
-    sum_qkv = jnp.stack(sum_pairs).reshape(pairs, share, owned, 3, 128)
-    sum_qkv = jnp.transpose(sum_qkv, (2, 3, 1, 0, 4)).reshape(owned, 3, share, wide)[..., :cols].reshape(owned, 3 * model)
+    if wide != cols:
+        sum_qkv = sum_qkv.reshape(owned, 3, share, wide)[..., :cols].reshape(owned, 3 * model)
     return (
         result,
         grad_tokens.astype(jnp.float32),

time: 340 us -> 333 us (0.979)
  local copies, waits for them, and re-layouts: 12.1 us -> 7.59 us
    another operation x4 -> x0, local copies, waits for them, and re-layouts: 3.54 us -> none  [the longest x3 2.74 us: shards(): sum_qkv = jnp.stack(sum_pairs).reshape(pairs, share, owned, 3, 128)]
where the time goes in v2:
time: 333 us; the launch traced here: 331 us
  Pallas kernels  318 us (95%)
  local copies, waits for them, and re-layouts  7.59 us (2%)
  other arithmetic  4.8 us (1%)
    pallas_call x1, Pallas kernels, last_half(): pl.pallas_call(functools.partial(last_kernel, sizes, block, pairs), grid=...  145 us
    pallas_call x1, Pallas kernels, first_half(): pl.pallas_call(functools.partial(first_kernel, sizes, block, pairs), grid...  120 us
    pallas_call x1, Pallas kernels, feed_forward(): pl.pallas_call(functools.partial(mlp_kernel, sizes, cols, tile, chunk), o...  52.9 us

profile of v2, /device:TPU:0, one launch (start us, length us, event | category | flops | bytes accessed | tf_op | source)
XLA Modules:
  0.0 331.3 jit_solution(11037876743828744583)
XLA Ops:
  0.7 0.7 multiply_bitcast_fusion
  1.3 0.7 maximum_convert_fusion
  2.0 0.4 dynamic_update_slice.6
  2.4 0.2 dynamic_update_slice.7.refs_2_
  2.7 0.0 copy-start.4
  2.7 1.0 reshape.50
  3.6 0.1 copy.22
  3.7 0.7 reshape.51.refs_3_
  4.4 0.0 copy-done.4
  4.5 120.0 %shard_map.186 = (bf16[2048,384]{1,0:T(8,128)(2,1)}, f32[3,8,2048]{2,1,0:T(8,128)}, bf16[2,1024,384]{2,1,0:T(8,128)(2,1)}, bf16[2,512,768]{2,1,0:T(8,128)(2,1)},...) custom-call(bf16[2,512,768]{2,1,0:T(8,128)(2,1)} %refs_0_.1, ...), custom_call_target="tpu_custom_call" | custom-call | tf_op jit(solution)/shard_map/pallas_call | solution.py:779
  124.4 52.9 %shard_map.187 = (bf16[2,512,768]{2,1,0:T(8,128)(2,1)}, bf16[2,1024,384]{2,1,0:T(8,128)(2,1)}, f32[1024,768]{1,0:T(8,128)}, bf16[768,768]{1,0:T(8,128)(2,1)}, bf...) custom-call(bf16[2,1024,384]{2,1,0:T(8,128)(2,1)} %get-tuple-element.35.refs_0_, ...), custom_call_target="tpu_custom_call" | custom-call | tf_op jit(solution)/shard_map/pallas_call | solution.py:1042
  177.4 145.0 %shard_map.188 = (f32[24,768]{1,0:T(8,128)}, f32[24,3072]{1,0:T(8,128)}, f32[96,768]{1,0:T(8,128)}, f32[24,2304]{1,0:T(8,128)}, bf16[2,512,768]{2,1,0:T(8,128)(2,1)}, /*index=5*/f32[8,768]{1,0:T(8,128)}) custom-call(bf16[2048,1152]{1,0:T(8,128)(2,1)} %get-tuple-element.43.refs_0_.refs_1_.refs_2_, ...), custom_call_target="tpu_custom_call" | custom-call | tf_op jit(solution)/shard_map/pallas_call | solution.py:1342
  322.4 0.8 constant_dynamic-slice_fusion
  323.2 0.5 slice_bitcast_fusion
  323.7 3.4 %convert_element_type.15 = f32[2,512,768]{2,1,0:T(8,128)} convert(bf16[2,512,768]{2,1,0:T(8,128)(2,1)} %get-tuple-element.54) | non-fusion elementwise | flops 786432 | bytes 4718592 | tf_op jit(solution)/shard_map/convert_element_type | solution.py:1449
  327.2 0.0 copy-done
  327.2 0.0 copy-start.1
  327.2 1.1 copy.30
  328.3 0.0 copy-done.3
  328.3 0.7 copy.31
  329.0 0.6 copy.32
  329.6 0.7 copy.33
  330.4 0.0 copy-done.1
  330.4 0.7 copy.34
  (7 shorter events, 0.0 us)
Async XLA Ops:
  2.7 1.8 copy-start.4
  323.7 3.4 %copy-start = (bf16[2,512,768]{2,1,0:T(8,128)(2,1)S(1)}, bf16[2,512,768]{2,1,0:T(8,128)(2,1)}, u32[]{:S(2)}) copy-start(bf16[2,512,768]{2,1,0:T(8,128)(2,1)} %get-tuple-element.74) | copy-start | bytes 4718596
  327.2 1.2 copy-start.3
  327.2 1.9 copy-start.5
  327.2 2.5 copy-start.2
  327.2 3.2 copy-start.1

commit v3 on v2

--- a/solution.py
+++ b/solution.py
@@ -1119,13 +1119,13 @@
             where = (14 + 2.7 * per * n) if t == 0 else (38 + 8 * t + 1.4 * per * n)
             tasks.append((where, functools.partial(fold.step, a, k, t)))
     for a in range(3):
-        tasks.append((72 + 2 * a, functools.partial(fold.total, a)))
+        tasks.append((80 + 2 * a, functools.partial(fold.total, a)))
     for p in range(pairs - 1):
         third = 85.0 / pairs
         for n, k in enumerate(fold.order):
             tasks.append(((p + 1.1) * third, functools.partial(fold.join, 3 + p, k)))
             for t in range(bits):
-                where = (68 if p == pairs - 2 else 60) + 6 * t
+                where = (74 if p == pairs - 2 else 64) + 5 * t
                 tasks.append((where, functools.partial(fold.step, 3 + p, k, t)))
     tasks = [(where / 85.0, call) for where, call in tasks]
     tasks.sort(key=lambda task: task[0])

time: 333 us -> 329 us (0.988)
  Pallas kernels: 318 us -> 314 us
    pallas_call x1, Pallas kernels: 145 us -> 141 us  [last_half(): pl.pallas_call(functools.partial(last_kernel, sizes, block, pairs), grid=...]
where the time goes in v3:
time: 329 us; the launch traced here: 327 us
  Pallas kernels  314 us (95%)
  local copies, waits for them, and re-layouts  7.59 us (2%)
  other arithmetic  4.8 us (1%)
    pallas_call x1, Pallas kernels, last_half(): pl.pallas_call(functools.partial(last_kernel, sizes, block, pairs), grid=...  141 us
    pallas_call x1, Pallas kernels, first_half(): pl.pallas_call(functools.partial(first_kernel, sizes, block, pairs), grid...  120 us
    pallas_call x1, Pallas kernels, feed_forward(): pl.pallas_call(functools.partial(mlp_kernel, sizes, cols, tile, chunk), o...  52.9 us

profile of v3, /device:TPU:0, one launch (start us, length us, event | category | flops | bytes accessed | tf_op | source)
XLA Modules:
  0.0 327.2 jit_solution(11439487015436520554)
XLA Ops:
  0.7 0.7 multiply_bitcast_fusion
  1.3 0.7 maximum_convert_fusion
  2.0 0.4 dynamic_update_slice.6
  2.4 0.2 dynamic_update_slice.7.refs_2_
  2.7 0.0 copy-start.4
  2.7 1.0 reshape.50
  3.6 0.1 copy.22
  3.7 0.7 reshape.51.refs_3_
  4.4 0.0 copy-done.4
  4.5 120.0 %shard_map.186 = (bf16[2048,384]{1,0:T(8,128)(2,1)}, f32[3,8,2048]{2,1,0:T(8,128)}, bf16[2,1024,384]{2,1,0:T(8,128)(2,1)}, bf16[2,512,768]{2,1,0:T(8,128)(2,1)},...) custom-call(bf16[2,512,768]{2,1,0:T(8,128)(2,1)} %refs_0_.1, ...), custom_call_target="tpu_custom_call" | custom-call | tf_op jit(solution)/shard_map/pallas_call | solution.py:779
  124.4 52.9 %shard_map.187 = (bf16[2,512,768]{2,1,0:T(8,128)(2,1)}, bf16[2,1024,384]{2,1,0:T(8,128)(2,1)}, f32[1024,768]{1,0:T(8,128)}, bf16[768,768]{1,0:T(8,128)(2,1)}, bf...) custom-call(bf16[2,1024,384]{2,1,0:T(8,128)(2,1)} %get-tuple-element.35.refs_0_, ...), custom_call_target="tpu_custom_call" | custom-call | tf_op jit(solution)/shard_map/pallas_call | solution.py:1042
  177.4 141.0 %shard_map.188 = (f32[24,768]{1,0:T(8,128)}, f32[24,3072]{1,0:T(8,128)}, f32[96,768]{1,0:T(8,128)}, f32[24,2304]{1,0:T(8,128)}, bf16[2,512,768]{2,1,0:T(8,128)(2,1)}, /*index=5*/f32[8,768]{1,0:T(8,128)}) custom-call(bf16[2048,1152]{1,0:T(8,128)(2,1)} %get-tuple-element.43.refs_0_.refs_1_.refs_2_, ...), custom_call_target="tpu_custom_call" | custom-call | tf_op jit(solution)/shard_map/pallas_call | solution.py:1342
  318.4 0.8 constant_dynamic-slice_fusion
  319.1 0.5 slice_bitcast_fusion
  319.7 3.4 %convert_element_type.15 = f32[2,512,768]{2,1,0:T(8,128)} convert(bf16[2,512,768]{2,1,0:T(8,128)(2,1)} %get-tuple-element.54) | non-fusion elementwise | flops 786432 | bytes 4718592 | tf_op jit(solution)/shard_map/convert_element_type | solution.py:1449
  323.1 0.0 copy-done
  323.1 0.0 copy-start.1
  323.1 1.1 copy.30
  324.3 0.0 copy-done.3
  324.3 0.7 copy.31
  325.0 0.0 copy-done.5
  325.0 0.6 copy.32
  325.6 0.7 copy.33
  326.3 0.7 copy.34
  (7 shorter events, 0.0 us)
Async XLA Ops:
  2.7 1.8 copy-start.4
  319.7 3.4 %copy-start = (bf16[2,512,768]{2,1,0:T(8,128)(2,1)S(1)}, bf16[2,512,768]{2,1,0:T(8,128)(2,1)}, u32[]{:S(2)}) copy-start(bf16[2,512,768]{2,1,0:T(8,128)(2,1)} %get-tuple-element.74) | copy-start | bytes 4718596
  323.1 1.2 copy-start.3
  323.1 1.9 copy-start.5
  323.1 2.5 copy-start.2
  323.1 3.2 copy-start.1

commit v4 on v3

--- a/solution.py
+++ b/solution.py
@@ -1119,13 +1119,13 @@
             where = (14 + 2.7 * per * n) if t == 0 else (38 + 8 * t + 1.4 * per * n)
             tasks.append((where, functools.partial(fold.step, a, k, t)))
     for a in range(3):
-        tasks.append((80 + 2 * a, functools.partial(fold.total, a)))
+        tasks.append((82 + a, functools.partial(fold.total, a)))
     for p in range(pairs - 1):
         third = 85.0 / pairs
         for n, k in enumerate(fold.order):
             tasks.append(((p + 1.1) * third, functools.partial(fold.join, 3 + p, k)))
             for t in range(bits):
-                where = (74 if p == pairs - 2 else 64) + 5 * t
+                where = (79 if p == pairs - 2 else 70) + 4 * t
                 tasks.append((where, functools.partial(fold.step, 3 + p, k, t)))
     tasks = [(where / 85.0, call) for where, call in tasks]
     tasks.sort(key=lambda task: task[0])

time: 329 us -> 329 us (level)
  no operation moved by 1% of the time
where the time goes in v4:
time: 329 us; the launch traced here: 327 us
  Pallas kernels  313 us (95%)
  local copies, waits for them, and re-layouts  7.59 us (2%)
  other arithmetic  4.8 us (1%)
    pallas_call x1, Pallas kernels, last_half(): pl.pallas_call(functools.partial(last_kernel, sizes, block, pairs), grid=...  141 us
    pallas_call x1, Pallas kernels, first_half(): pl.pallas_call(functools.partial(first_kernel, sizes, block, pairs), grid...  120 us
    pallas_call x1, Pallas kernels, feed_forward(): pl.pallas_call(functools.partial(mlp_kernel, sizes, cols, tile, chunk), o...  52.9 us

profile of v4, /device:TPU:0, one launch (start us, length us, event | category | flops | bytes accessed | tf_op | source)
XLA Modules:
  0.0 326.8 jit_solution(2048465954466907367)
XLA Ops:
  0.7 0.7 multiply_bitcast_fusion
  1.3 0.7 maximum_convert_fusion
  2.0 0.4 dynamic_update_slice.6
  2.4 0.2 dynamic_update_slice.7.refs_2_
  2.7 0.0 copy-start.4
  2.7 1.0 reshape.50
  3.6 0.1 copy.22
  3.7 0.7 reshape.51.refs_3_
  4.4 0.0 copy-done.4
  4.5 120.0 %shard_map.186 = (bf16[2048,384]{1,0:T(8,128)(2,1)}, f32[3,8,2048]{2,1,0:T(8,128)}, bf16[2,1024,384]{2,1,0:T(8,128)(2,1)}, bf16[2,512,768]{2,1,0:T(8,128)(2,1)},...) custom-call(bf16[2,512,768]{2,1,0:T(8,128)(2,1)} %refs_0_.1, ...), custom_call_target="tpu_custom_call" | custom-call | tf_op jit(solution)/shard_map/pallas_call | solution.py:779
  124.4 52.9 %shard_map.187 = (bf16[2,512,768]{2,1,0:T(8,128)(2,1)}, bf16[2,1024,384]{2,1,0:T(8,128)(2,1)}, f32[1024,768]{1,0:T(8,128)}, bf16[768,768]{1,0:T(8,128)(2,1)}, bf...) custom-call(bf16[2,1024,384]{2,1,0:T(8,128)(2,1)} %get-tuple-element.35.refs_0_, ...), custom_call_target="tpu_custom_call" | custom-call | tf_op jit(solution)/shard_map/pallas_call | solution.py:1042
  177.4 140.6 %shard_map.188 = (f32[24,768]{1,0:T(8,128)}, f32[24,3072]{1,0:T(8,128)}, f32[96,768]{1,0:T(8,128)}, f32[24,2304]{1,0:T(8,128)}, bf16[2,512,768]{2,1,0:T(8,128)(2,1)}, /*index=5*/f32[8,768]{1,0:T(8,128)}) custom-call(bf16[2048,1152]{1,0:T(8,128)(2,1)} %get-tuple-element.43.refs_0_.refs_1_.refs_2_, ...), custom_call_target="tpu_custom_call" | custom-call | tf_op jit(solution)/shard_map/pallas_call | solution.py:1342
  318.0 0.8 constant_dynamic-slice_fusion
  318.7 0.5 slice_bitcast_fusion
  319.3 3.4 %convert_element_type.15 = f32[2,512,768]{2,1,0:T(8,128)} convert(bf16[2,512,768]{2,1,0:T(8,128)(2,1)} %get-tuple-element.54) | non-fusion elementwise | flops 786432 | bytes 4718592 | tf_op jit(solution)/shard_map/convert_element_type | solution.py:1449
  322.7 0.0 copy-done
  322.7 0.0 copy-start.1
  322.7 1.1 copy.30
  323.9 0.0 copy-done.3
  323.9 0.7 copy.31
  324.6 0.0 copy-done.5
  324.6 0.6 copy.32
  325.2 0.7 copy.33
  325.9 0.7 copy.34
  (7 shorter events, 0.0 us)
Async XLA Ops:
  2.7 1.8 copy-start.4
  319.3 3.4 %copy-start = (bf16[2,512,768]{2,1,0:T(8,128)(2,1)S(1)}, bf16[2,512,768]{2,1,0:T(8,128)(2,1)}, u32[]{:S(2)}) copy-start(bf16[2,512,768]{2,1,0:T(8,128)(2,1)} %get-tuple-element.74) | copy-start | bytes 4718596
  322.7 1.2 copy-start.3
  322.7 1.9 copy-start.5
  322.7 2.5 copy-start.2
  322.7 3.2 copy-start.1
